TPU v7x, 32 devices: a whole 2x2x4 slice. The times are simulated.
32 devices in a mesh: section: 2 (over core), seq: 4 (over z), wt: 4 (over y, x).
Axes of the slice: x: 2, y: 2, z: 4, core: 2. Of those that a mesh axis runs over, the one named last changes fastest.
Arguments:
- block_input: bfloat16 [2, 4, 256, 1024], P(None, 'wt', 'seq'), may hold values from -6 to 6
- positions: int32 [2, 4, 256], P(None, 'wt', 'seq'), may hold values from 0 to 255, as said below
- cotangent: bfloat16 [2, 4, 256, 1024], P(None, 'wt', 'seq'), may hold values from -6 to 6
- norm_gain: float32 [2, 1024], P('section'), may hold values from 0.5 to 1.5
- in_weight: bfloat16 [2, 1024, 4384], P('section', 'wt'), may hold values from -0.1875 to 0.1875
- conv_weight: float32 [2, 4, 2304], P('section'), may hold values from -3 to 3
- conv_bias: float32 [2, 2304], P('section'), may hold values from -3 to 3
- dt_bias: float32 [2, 32], P('section'), may hold values from -9 to -3
- a_log: float32 [2, 32], P('section'), may hold values from -2.3 to 1
- skip_d: float32 [2, 32], P('section'), may hold values from 0.5 to 1.5
- gate_gain: float32 [2, 2048], P('section'), may hold values from 0.5 to 1.5
- out_weight: bfloat16 [2, 2048, 1024], P('section', 'wt'), may hold values from -0.125 to 0.125
Outputs:
- section_out: bfloat16 [2, 2, 4, 256, 1024], P('section', None, 'wt', 'seq')
- input_grad: float32 [2, 2, 4, 256, 1024], P('section', None, 'wt', 'seq')
- grad_norm_gain: float32 [2, 1024], P('section')
- grad_in_weight: float32 [2, 1024, 4384], P('section', 'wt')
- grad_conv_weight: float32 [2, 4, 2304], P('section')
- grad_conv_bias: float32 [2, 2304], P('section')
- grad_dt_bias: float32 [2, 32], P('section')
- grad_a_log: float32 [2, 32], P('section')
- grad_skip_d: float32 [2, 32], P('section')
- grad_gate_gain: float32 [2, 2048], P('section')
- grad_out_weight: float32 [2, 2048, 1024], P('section', 'wt')
Inputs may be any that keep to these rules, and one draw needn't show every extreme that they name: `positions`: each row begins a document at its first token and holds one to three documents; a position counts the tokens before it in its document. Some row holds a single document.
All inputs are finite; a program needn't handle non-finite values.
Results may differ from a plain program's by a relative error of at most 0.018.
Values may be sent and summed in bfloat16 or wider, within the bound.
A program may use at most 192 MiB of HBM per device.

v0:
```python
import jax
import jax.numpy as jnp
from jax import lax
from jax.sharding import PartitionSpec as P

H = 32
P_SIZE = 64
N = 128
K = 4
SPAN = 256
DI = 2048


EPSILON = 1e-05
HIGHEST = lax.Precision.HIGHEST
CONTRACT_ROWS = (((0,), (0,)), ((), ()))
CONTRACT_COLS = (((1,), (1,)), ((), ()))


def from_behind(block, axis, distance):
    devices = range(lax.axis_size(axis))
    route = [(i - distance, i) for i in devices if i - distance in devices]
    return lax.ppermute(block, axis, route)


def swish_slope(value):
    sigma = jax.nn.sigmoid(value)
    return sigma * (1.0 + value * (1.0 - sigma))


def lagged(channels, offset):
    return jnp.concatenate(
        [jnp.zeros((offset, channels.shape[1]), channels.dtype), channels[:-offset]], 0
    )


def leading_rows(channels, offset):
    return jnp.concatenate(
        [channels[offset:], jnp.zeros((offset, channels.shape[1]), channels.dtype)], 0
    )


def convolve(channels, weights, biases, places):
    values = channels.astype(jnp.float32)
    total = biases + values * weights[0]
    for offset in range(1, weights.shape[0]):
        total = total + jnp.where(
            (places >= offset)[:, None], lagged(values, offset) * weights[offset], 0.0
        )
    return total


def convolve_back(grad_pre, channels, weights, places):
    values = channels.astype(jnp.float32)
    weight_rows = [jnp.sum(grad_pre * values, axis=0)]
    grad_chan = grad_pre * weights[0]
    for offset in range(1, weights.shape[0]):
        masked = jnp.where((places >= offset)[:, None], grad_pre, 0.0)
        weight_rows.append(jnp.sum(masked * lagged(values, offset), axis=0))
        grad_chan = grad_chan + leading_rows(masked * weights[offset], offset)
    return (grad_chan, jnp.stack(weight_rows), jnp.sum(grad_pre, axis=0))


def block_tables(doc_start):
    spans = doc_start.shape[0] // SPAN
    starts = doc_start.reshape(spans, SPAN)
    inside = lax.iota(jnp.int32, SPAN)
    causal = (inside[:, None] >= inside[None, :])[None] & (starts[:, :, None] == starts[:, None, :])
    at_end = starts == starts[:, -1:]
    at_start = starts == starts[:, :1]
    blocks = lax.iota(jnp.int32, spans)
    between = (
        (blocks[None, :, None] < blocks[None, None, :])
        & (blocks[None, None, :] < blocks[:, None, None])
    ).astype(jnp.float32)
    across = (starts[None, :, -1] == starts[:, 0][:, None]) & (blocks[None, :] < blocks[:, None])
    return (causal, at_end, at_start, between, across)


def scan_values(x_blocks, b_blocks, c_blocks, step_heads, rates, tables):
    causal, at_end, at_start, between, across = tables
    cumul = jnp.cumsum(step_heads * rates[None, :, None], axis=2)
    spread = cumul[:, :, :, None] - cumul[:, :, None, :]
    inner_mask = causal[:, None]
    decay = jnp.where(inner_mask, jnp.exp(jnp.where(inner_mask, spread, 0.0)), 0.0)
    tail = jnp.where(at_end[:, None], jnp.exp(cumul[:, :, -1:] - cumul), 0.0)
    leading = jnp.where(at_start[:, None], jnp.exp(cumul), 0.0)
    segment = jnp.einsum("kh,cdk->hcd", cumul[:, :, -1], between, precision=HIGHEST)
    mixing = jnp.where(across[None], jnp.exp(jnp.where(across[None], segment, 0.0)), 0.0)
    scores = jnp.einsum("cln,csn->cls", c_blocks, b_blocks, preferred_element_type=jnp.float32)
    weights = (scores[:, None] * decay * step_heads[:, :, None, :]).astype(jnp.bfloat16)
    inflow_scale = jnp.swapaxes(step_heads * tail, 1, 2)[..., None]
    inflow = (x_blocks * inflow_scale).astype(jnp.bfloat16)
    state = jnp.einsum("csn,cshp->chnp", b_blocks, inflow, preferred_element_type=jnp.float32)
    carried = jnp.einsum("hcd,dhnp->chnp", mixing, state, precision=HIGHEST).astype(jnp.bfloat16)
    readout = jnp.einsum("cln,chnp->clhp", c_blocks, carried, preferred_element_type=jnp.float32)
    lead_rows = jnp.swapaxes(leading, 1, 2)[..., None]
    return (
        decay,
        tail,
        mixing,
        scores,
        weights,
        inflow_scale,
        inflow,
        state,
        carried,
        readout,
        lead_rows,
    )


def mixer_parts(channels, step_raw, places, columns, biases, step_bias):
    width = step_raw.shape[1]
    length = channels.shape[0]
    spans = length // SPAN
    pre_act = convolve(channels, columns, biases, places)
    act = jax.nn.silu(pre_act).astype(jnp.bfloat16)
    x_blocks = act[:, : width * P_SIZE].reshape(spans, SPAN, width, P_SIZE)
    b_blocks = act[:, width * P_SIZE : width * P_SIZE + N].reshape(spans, SPAN, N)
    c_blocks = act[:, width * P_SIZE + N :].reshape(spans, SPAN, N)
    steps = jax.nn.softplus(step_raw.astype(jnp.float32) + step_bias)
    step_heads = jnp.swapaxes(steps.reshape(spans, SPAN, width), 1, 2)
    tables = block_tables(lax.iota(jnp.int32, length) - places)
    return (pre_act, x_blocks, b_blocks, c_blocks, step_heads, tables)


def mixer_forward(channels, step_raw, places, heads):
    columns, biases, step_bias, rates, skips = heads
    pre_act, x_blocks, b_blocks, c_blocks, step_heads, tables = mixer_parts(
        channels, step_raw, places, columns, biases, step_bias
    )
    values = scan_values(x_blocks, b_blocks, c_blocks, step_heads, rates, tables)
    weights, readout, lead_rows = (values[4], values[9], values[10])
    local = jnp.einsum("chls,cshp->clhp", weights, x_blocks, preferred_element_type=jnp.float32)
    mixed = local + readout * lead_rows + skips[None, None, :, None] * x_blocks
    return mixed.reshape(channels.shape[0], step_raw.shape[1] * P_SIZE)


def mixer_backward(grad_heads, channels, step_raw, places, heads):
    columns, biases, step_bias, rates, skips = heads
    pre_act, x_blocks, b_blocks, c_blocks, step_heads, tables = mixer_parts(
        channels, step_raw, places, columns, biases, step_bias
    )
    (
        decay,
        tail,
        mixing,
        scores,
        weights,
        inflow_scale,
        inflow,
        state,
        carried,
        readout,
        lead_rows,
    ) = scan_values(x_blocks, b_blocks, c_blocks, step_heads, rates, tables)
    between = tables[3]
    width = step_raw.shape[1]
    length = channels.shape[0]
    grad_y = grad_heads.reshape(x_blocks.shape)
    grad_float = grad_y.astype(jnp.float32)
    grad_skip = jnp.sum(grad_float * x_blocks, axis=(0, 1, 3))
    grad_x = skips[None, None, :, None] * grad_float
    grad_cumul = jnp.swapaxes(jnp.sum(grad_float * readout * lead_rows, axis=3), 1, 2)
    grad_readout = (grad_float * lead_rows).astype(jnp.bfloat16)
    grad_c = jnp.einsum("clhp,chnp->cln", grad_readout, carried, preferred_element_type=jnp.float32)
    grad_carried = jnp.einsum(
        "cln,clhp->chnp", c_blocks, grad_readout, preferred_element_type=jnp.float32
    )
    grad_state = jnp.einsum("hcd,chnp->dhnp", mixing, grad_carried, precision=HIGHEST).astype(
        jnp.bfloat16
    )
    grad_mixing = jnp.einsum("chnp,dhnp->hcd", grad_carried, state, precision=HIGHEST)
    grad_total = jnp.einsum("hcd,cdk->kh", grad_mixing * mixing, between, precision=HIGHEST)
    grad_b = jnp.einsum("cshp,chnp->csn", inflow, grad_state, preferred_element_type=jnp.float32)
    grad_inflow = jnp.einsum(
        "csn,chnp->cshp", b_blocks, grad_state, preferred_element_type=jnp.float32
    )
    grad_x = grad_x + grad_inflow * inflow_scale
    through_x = jnp.swapaxes(jnp.sum(grad_inflow * x_blocks, axis=3), 1, 2)
    grad_step = through_x * tail
    through_tail = through_x * step_heads * tail
    grad_cumul = grad_cumul - through_tail
    grad_cumul = grad_cumul.at[:, :, -1].add(jnp.sum(through_tail, axis=2) + grad_total)
    grad_weights = jnp.einsum(
        "clhp,cshp->chls", grad_y, x_blocks, preferred_element_type=jnp.float32
    )
    grad_x = grad_x + jnp.einsum(
        "chls,clhp->cshp", weights, grad_y, preferred_element_type=jnp.float32
    )
    through_decay = grad_weights * decay
    grad_scores = jnp.sum(through_decay * step_heads[:, :, None, :], axis=1).astype(jnp.bfloat16)
    with_scores = through_decay * scores[:, None]
    grad_step = grad_step + jnp.sum(with_scores, axis=2)
    paired = with_scores * step_heads[:, :, None, :]
    grad_cumul = grad_cumul + jnp.sum(paired, axis=3) - jnp.sum(paired, axis=2)
    grad_c = grad_c + jnp.einsum(
        "cls,csn->cln", grad_scores, b_blocks, preferred_element_type=jnp.float32
    )
    grad_b = grad_b + jnp.einsum(
        "cls,cln->csn", grad_scores, c_blocks, preferred_element_type=jnp.float32
    )
    grad_decay_log = jnp.flip(jnp.cumsum(jnp.flip(grad_cumul, 2), axis=2), 2)
    grad_step = grad_step + grad_decay_log * rates[None, :, None]
    grad_rate = jnp.sum(grad_decay_log * step_heads, axis=(0, 2))
    grad_act = jnp.concatenate(
        [
            grad_x.reshape(length, width * P_SIZE),
            grad_b.reshape(length, N),
            grad_c.reshape(length, N),
        ],
        1,
    )
    grad_pre = grad_act * swish_slope(pre_act)
    grad_chan, grad_columns, grad_biases = convolve_back(grad_pre, channels, columns, places)
    grad_step_raw = jnp.swapaxes(grad_step, 1, 2).reshape(length, width) * jax.nn.sigmoid(
        step_raw.astype(jnp.float32) + step_bias
    )
    head_grads = (
        grad_columns,
        grad_biases,
        jnp.sum(grad_step_raw, axis=0),
        grad_rate * rates,
        grad_skip,
    )
    return (grad_chan, grad_step_raw, head_grads)


def head_params(conv_weight, conv_bias, dt_bias, a_log, skip_d):
    width = H // lax.axis_size("seq")
    first = lax.axis_index("seq") * width
    columns = jnp.concatenate(
        [
            lax.dynamic_slice_in_dim(conv_weight, first * P_SIZE, width * P_SIZE, 1),
            conv_weight[:, DI:],
        ],
        1,
    )
    biases = jnp.concatenate(
        [lax.dynamic_slice_in_dim(conv_bias, first * P_SIZE, width * P_SIZE, 0), conv_bias[DI:]], 0
    )
    step_bias = lax.dynamic_slice_in_dim(dt_bias, first, width, 0)
    rates = -jnp.exp(lax.dynamic_slice_in_dim(a_log, first, width, 0))
    skips = lax.dynamic_slice_in_dim(skip_d, first, width, 0)
    return (columns, biases, step_bias, rates, skips)


def place_heads(head_grads):
    grad_columns, grad_biases, grad_step_bias, grad_rate_log, grad_skip = head_grads
    width = grad_step_bias.shape[0]
    first = lax.axis_index("seq") * width
    weight_full = jnp.concatenate(
        [
            lax.dynamic_update_slice_in_dim(
                jnp.zeros((K, DI), jnp.float32),
                grad_columns[:, : width * P_SIZE],
                first * P_SIZE,
                1,
            ),
            grad_columns[:, width * P_SIZE :],
        ],
        1,
    )
    bias_full = jnp.concatenate(
        [
            lax.dynamic_update_slice_in_dim(
                jnp.zeros((DI,), jnp.float32), grad_biases[: width * P_SIZE], first * P_SIZE, 0
            ),
            grad_biases[width * P_SIZE :],
        ],
        0,
    )
    spread_out = [
        lax.dynamic_update_slice_in_dim(jnp.zeros((H,), jnp.float32), member, first, 0)
        for member in (grad_step_bias, grad_rate_log, grad_skip)
    ]
    return (weight_full, bias_full, spread_out[0], spread_out[1], spread_out[2])


def forward_tick(inputs, places, w_in, w_out, gain, gate, heads):
    section_in = inputs.astype(jnp.float32)
    scale = lax.rsqrt(jnp.mean(section_in * section_in, axis=-1, keepdims=True) + EPSILON)
    normed = (section_in * scale * gain).astype(jnp.bfloat16)
    proj = jnp.dot(normed, w_in, preferred_element_type=jnp.float32)
    z_gate = proj[:, :DI]
    sent = proj[:, DI:].astype(jnp.bfloat16)
    x_heads, step_raw = (
        lax.all_to_all(sent[:, :DI], "seq", split_axis=1, concat_axis=0, tiled=True),
        lax.all_to_all(sent[:, DI + 2 * N :], "seq", split_axis=1, concat_axis=0, tiled=True),
    )
    bc_full = lax.all_gather(sent[:, DI : DI + 2 * N], "seq", axis=0, tiled=True)
    channels = jnp.concatenate([x_heads, bc_full], 1)
    mixed = mixer_forward(channels, step_raw, places, heads)
    y_tok = lax.all_to_all(
        mixed.astype(jnp.bfloat16), "seq", split_axis=0, concat_axis=1, tiled=True
    )
    gated = y_tok.astype(jnp.float32) * jax.nn.silu(z_gate)
    gate_scale = lax.rsqrt(jnp.mean(gated * gated, axis=-1, keepdims=True) + EPSILON)
    normed_out = (gated * gate_scale * gate).astype(jnp.bfloat16)
    result = (section_in + jnp.dot(normed_out, w_out, preferred_element_type=jnp.float32)).astype(
        jnp.bfloat16
    )
    kept = (
        inputs,
        scale,
        normed,
        z_gate,
        channels,
        step_raw,
        y_tok,
        gate_scale,
        normed_out,
        places,
    )
    return (result, kept)


def backward_tick(grad_out, kept, w_in, w_out, gain, gate, heads):
    inputs, scale, normed, z_gate, channels, step_raw, y_tok, gate_scale, normed_out, places = kept
    grad_low = grad_out.astype(jnp.bfloat16)
    grad_w_out = lax.dot_general(
        normed_out, grad_low, CONTRACT_ROWS, preferred_element_type=jnp.float32
    )
    grad_normed_out = lax.dot_general(
        grad_low, w_out, CONTRACT_COLS, preferred_element_type=jnp.float32
    )
    y_float = y_tok.astype(jnp.float32)
    z_swish = jax.nn.silu(z_gate)
    gated = y_float * z_swish
    grad_gate = jnp.sum(grad_normed_out * gated * gate_scale, axis=0)
    scaled_grad = grad_normed_out * gate
    grad_gated = gate_scale * (
        scaled_grad
        - gated * gate_scale * gate_scale * jnp.mean(scaled_grad * gated, axis=-1, keepdims=True)
    )
    grad_y = (grad_gated * z_swish).astype(jnp.bfloat16)
    grad_z = grad_gated * y_float * swish_slope(z_gate)
    grad_heads = lax.all_to_all(grad_y, "seq", split_axis=1, concat_axis=0, tiled=True)
    grad_chan, grad_step_raw, head_grads = mixer_backward(
        grad_heads, channels, step_raw, places, heads
    )
    width = step_raw.shape[1]
    back_x, back_step = (
        lax.all_to_all(
            grad_chan[:, : width * P_SIZE].astype(jnp.bfloat16),
            "seq",
            split_axis=0,
            concat_axis=1,
            tiled=True,
        ),
        lax.all_to_all(
            grad_step_raw.astype(jnp.bfloat16), "seq", split_axis=0, concat_axis=1, tiled=True
        ),
    )
    back_bc = lax.psum_scatter(
        grad_chan[:, width * P_SIZE :].astype(jnp.bfloat16), "seq", scatter_dimension=0, tiled=True
    )
    grad_proj = jnp.concatenate([grad_z.astype(jnp.bfloat16), back_x, back_bc, back_step], 1)
    grad_w_in = lax.dot_general(
        normed, grad_proj, CONTRACT_ROWS, preferred_element_type=jnp.float32
    )
    grad_normed = lax.dot_general(
        grad_proj, w_in, CONTRACT_COLS, preferred_element_type=jnp.float32
    )
    section_in = inputs.astype(jnp.float32)
    grad_gain = jnp.sum(grad_normed * section_in * scale, axis=0)
    scaled_in = grad_normed * gain
    grad_in = grad_out + scale * (
        scaled_in
        - section_in * scale * scale * jnp.mean(scaled_in * section_in, axis=-1, keepdims=True)
    )
    return (grad_in, grad_w_in, grad_w_out, (grad_gain, grad_gate) + head_grads)


def body(
    block_input,
    positions,
    cotangent,
    norm_gain,
    in_weight,
    conv_weight,
    conv_bias,
    dt_bias,
    a_log,
    skip_d,
    gate_gain,
    out_weight,
):
    w_in, w_out = (
        lax.all_gather(in_weight[0], "wt", axis=0, tiled=True),
        lax.all_gather(out_weight[0], "wt", axis=0, tiled=True),
    )
    places_all = lax.all_gather(positions, "seq", axis=2, tiled=True)
    gain = norm_gain[0]
    gate = gate_gain[0]
    heads = head_params(conv_weight[0], conv_bias[0], dt_bias[0], a_log[0], skip_d[0])
    first_section = lax.axis_index("section") == 0
    batches = block_input.shape[0]
    received = jnp.zeros(block_input.shape[2:], jnp.bfloat16)
    kept_ticks = []
    out_ticks = []
    for step_index in range(batches + 1):
        fresh = block_input[min(step_index, batches - 1), 0]
        inputs = jnp.where(first_section, fresh, received)
        places = jnp.where(
            first_section,
            places_all[min(step_index, batches - 1), 0],
            places_all[max(step_index - 1, 0), 0],
        )
        result, kept = forward_tick(inputs, places, w_in, w_out, gain, gate, heads)
        kept_ticks.append(kept)
        out_ticks.append(result)
        if step_index < batches:
            received = from_behind(result, "section", 1)
    grad_recv = jnp.zeros(block_input.shape[2:], jnp.float32)
    grad_ticks = []
    sum_in = jnp.zeros(w_in.shape, jnp.float32)
    sum_out = jnp.zeros(w_out.shape, jnp.float32)
    small_totals = None
    for step_index in range(batches + 1):
        if step_index < batches:
            from_loss = cotangent[step_index, 0].astype(jnp.float32)
        else:
            from_loss = jnp.zeros(block_input.shape[2:], jnp.float32)
        grad_out = jnp.where(first_section, grad_recv, from_loss)
        chosen = jax.tree.map(
            lambda early, later: jnp.where(first_section, early, later),
            kept_ticks[max(step_index - 1, 0)],
            kept_ticks[min(step_index + 1, batches)],
        )
        grad_in, grad_w_in, grad_w_out, smalls = backward_tick(
            grad_out, chosen, w_in, w_out, gain, gate, heads
        )
        grad_ticks.append(grad_in)
        sum_in = sum_in + grad_w_in
        sum_out = sum_out + grad_w_out
        small_totals = (
            smalls if small_totals is None else jax.tree.map(jnp.add, small_totals, smalls)
        )
        if step_index < batches:
            grad_recv = from_behind(grad_in.astype(jnp.bfloat16), "section", -1).astype(
                grad_in.dtype
            )
    shard_in, shard_out = (
        lax.psum_scatter(sum_in.astype(jnp.bfloat16), "wt", scatter_dimension=0, tiled=True).astype(
            jnp.float32
        ),
        lax.psum_scatter(
            sum_out.astype(jnp.bfloat16), "wt", scatter_dimension=0, tiled=True
        ).astype(jnp.float32),
    )
    total_in, total_out = (
        lax.psum(shard_in.astype(jnp.bfloat16), "seq").astype(jnp.float32),
        lax.psum(shard_out.astype(jnp.bfloat16), "seq").astype(jnp.float32),
    )
    grad_gain, grad_gate = (small_totals[0], small_totals[1])
    weight_full, bias_full, step_full, rate_full, skip_full = place_heads(small_totals[2:])
    summed = lax.psum(
        (grad_gain, grad_gate, weight_full, bias_full, step_full, rate_full, skip_full),
        ("seq", "wt"),
    )
    section_rows = jnp.stack(
        [
            jnp.where(first_section, out_ticks[index], out_ticks[index + 1])
            for index in range(batches)
        ]
    )
    grad_rows = jnp.stack(
        [
            jnp.where(first_section, grad_ticks[index + 1], grad_ticks[index])
            for index in range(batches)
        ]
    )
    return (
        section_rows[None, :, None],
        grad_rows[None, :, None],
        summed[0][None],
        total_in[None],
        summed[2][None],
        summed[3][None],
        summed[4][None],
        summed[5][None],
        summed[6][None],
        summed[1][None],
        total_out[None],
    )


def solution(mesh):
    placed = (
        P(None, "wt", "seq", None),
        P(None, "wt", "seq"),
        P(None, "wt", "seq", None),
        P("section", None),
        P("section", "wt", None),
        P("section", None, None),
        P("section", None),
        P("section", None),
        P("section", None),
        P("section", None),
        P("section", None),
        P("section", "wt", None),
    )
    return jax.shard_map(
        body,
        mesh=mesh,
        in_specs=placed,
        out_specs=(
            P("section", None, "wt", "seq", None),
            P("section", None, "wt", "seq", None),
            P("section", None),
            P("section", "wt", None),
            P("section", None, None),
            P("section", None),
            P("section", None),
            P("section", None),
            P("section", None),
            P("section", None),
            P("section", "wt", None),
        ),
        check_vma=False,
    )
```

profile of v0, /device:TPU:0, one launch (start us, length us, event | category | flops | bytes accessed | tf_op | source)
XLA Modules:
  0.0 905.9 jit_solution(16759661762547901851)
XLA Ops:
  8.9 15.0 %all_gather.20 = s32[2,1,256]{0,1,2:T(1,128)S(1)} all-gather(s32[2,1,64]{0,1,2:T(1,128)S(1)} %copy.498), channel_id=1, replica_groups=mesh['section'=2,'seq'=4,'wt'=4] {'seq'}, dimensions={2}, use_global_device_ids=true | all-gather | bytes 2560 | tf_op jit(solution)/shard_map/all_gather | solution.py:394
  23.9 4.9 fusion.366
  28.8 33.6 %fusion.371 = (s32[256]{0:T(256)}, s32[1,1,256]{0,1,2:T(1,128)}, s32[256]{0:T(256)}, s32[1,1,256]{0,1,2:T(1,128)}, s32[256]{0:T(256)S(1)}, /*index=5*/s32[256]{0...) fusion(s32[2,1,256]{0,1,2:T(1,128)S(1)} %all_gather.20, pred[]{:T(512)S(6)} %eq.285, ...), kind=kLoop, calls=%fused_computation.752 | loop fusion | flops 1792 | bytes 12289 | tf_op jit(solution)/shard_map/sub | solution.py:124
  71.9 22.1 %compare_reduce_fusion.6 = (pred[256]{0:T(512)(128)(4,1)}, pred[256]{0:T(512)(128)(4,1)S(1)}, pred[256]{0:T(512)(128)(4,1)S(1)}, pred[256]{0:T(512)(128)(4,1)}) fusion(s32[]{:T(128)} %bitcast.107, s32[2,1,256]{0,1,2:T(1,128)S(1)} %all_gather.20, s32[]{:T(128)} %bitcast.36, s32[]{:T(128)} %bitcast.22, s32[]{:T(128)} %bitcast.93), kind=kLoop, calls=%fused_computation.260 | loop fusion | flops 1536 | bytes 3088 | tf_op jit(solution)/shard_map/eq | solution.py:70
  95.5 9.5 %all-gather.5.cloned.1.call-done = bf16[1,1024,4384]{1,2,0:T(8,128)(2,1)} async-done(((bf16[1,256,4384]{1,2,0:T(8,128)(2,1)}), bf16[1,1024,4384]{1,2,0:T(8,128)(2,1)}) %all-gather.5.cloned.1.call-update) | async-done | bytes 8978448 | tf_op jit(solution)/shard_map/all_gather | solution.py:391
  105.0 6.4 fusion.385
  112.4 4.6 all-to-all-start.1
  117.0 13.9 %all_gather.19 = bf16[256,256]{1,0:T(8,128)(2,1)S(1)} all-gather(bf16[64,256]{1,0:T(8,128)(2,1)S(1)} %slice.607), channel_id=1, replica_groups=mesh['section'=2,'seq'=4,'wt'=4] {'seq'}, dimensions={0}, use_global_device_ids=true | all-gather | bytes 163840 | tf_op jit(solution)/shard_map/all_gather | solution.py:292
  131.8 4.5 all-to-all-start
  138.1 4.9 all-to-all-done
  149.8 3.7 all-to-all-start.2
  153.5 20.9 %compare_reduce_fusion = (pred[256]{0:T(512)(128)(4,1)}, pred[256]{0:T(512)(128)(4,1)}, pred[256]{0:T(512)(128)(4,1)S(1)}, pred[256]{0:T(512)(128)(4,1)S(1)}) fusion(s32[1,1,256]{0,1,2:T(1,128)S(1)} %copy-done.93, s32[]{:T(128)} %bitcast.263, s32[]{:T(128)} %bitcast.247, s32[]{:T(128)} %bitcast.59, s32[]{:T(128)} %bitcast.73, ...), kind=kLoop, calls=%fused_computation.254 | loop fusion | flops 1280 | bytes 3088 | tf_op jit(solution)/shard_map/eq | solution.py:69
  181.7 6.5 fusion.386
  189.0 5.1 all-to-all-start.4
  194.1 14.0 %all_gather.22 = bf16[256,256]{1,0:T(8,128)(2,1)S(1)} all-gather(bf16[64,256]{1,0:T(8,128)(2,1)S(1)} %slice.629), channel_id=1, replica_groups=mesh['section'=2,'seq'=4,'wt'=4] {'seq'}, dimensions={0}, use_global_device_ids=true | all-gather | bytes 163840 | tf_op jit(solution)/shard_map/all_gather | solution.py:292
  208.9 4.7 all-to-all-start.3
  215.4 4.9 all-to-all-done.3
  229.8 3.9 all-to-all-start.5
  233.7 21.5 %compare_reduce_fusion.2 = (pred[256]{0:T(512)(128)(4,1)}, pred[256]{0:T(512)(128)(4,1)}, pred[256]{0:T(512)(128)(4,1)}, pred[256]{0:T(512)(128)(4,1)}) fusion(s32[1,1,256]{0,1,2:T(1,128)S(1)} %copy-done.95, s32[]{:T(128)} %bitcast.199, s32[]{:T(128)} %bitcast.183, s32[1,1,256]{0,1,2:T(1,128)S(1)} %copy-done.96, s32[]{:T(128)} %bitcast.119, s32[]{:T(128)} %bitcast.135), kind=kLoop, calls=%fused_computation.256 | loop fusion | flops 1024 | bytes 3088 | tf_op jit(solution)/shard_map/eq | solution.py:69
  260.7 4.5 fusion.161
  269.8 5.1 all-to-all-start.7
  274.9 14.6 %all_gather.23 = bf16[256,256]{1,0:T(8,128)(2,1)} all-gather(bf16[64,256]{1,0:T(8,128)(2,1)S(1)} %slice.644), channel_id=1, replica_groups=mesh['section'=2,'seq'=4,'wt'=4] {'seq'}, dimensions={0}, use_global_device_ids=true | all-gather | bytes 163840 | tf_op jit(solution)/shard_map/all_gather | solution.py:292
  290.3 4.6 all-to-all-start.6
  345.1 5.1 all-to-all-start.8
  350.2 4.4 multiply_convert_fusion.12
  370.9 5.5 all-to-all-start.9
  417.9 3.8 all-to-all-start.11
  429.3 5.0 all-to-all-start.10
  450.5 6.2 fusion.139
  463.3 4.7 multiply_reduce_fusion.25
  470.9 5.1 all-to-all-start.12
  479.6 5.3 all-to-all-done.12
  519.7 3.8 all-to-all-start.14
  529.9 5.1 all-to-all-start.13
  542.7 3.8 all-to-all-done.13
  550.3 6.2 fusion.147
  569.3 5.6 fusion.159
  574.9 4.0 all-to-all-done.15
  596.0 9.1 %add_convert_fusion.1 = bf16[2048,1024]{1,0:T(8,128)(2,1)} fusion(f32[2048,1024]{1,0:T(8,128)} %fusion.161, f32[2048,1024]{1,0:T(8,128)} %fusion.159, bf16[64,2048]{1,0:T(8,128)(2,1)S(1)} %copy-done.36, bf16[64,2048]{1,0:T(8,128)(2,1)S(1)} %copy-done.34, pred[]{:T(512)S(6)} %eq.285, bf16[64,1024]{1,0:T(8,128)(2,1)S(1)} %copy-done.77), kind=kOutput, calls=%fused_computation.13 | convolution fusion | flops 275054592 | bytes 21626880 | tf_op jit(solution)/shard_map/dot_general | solution.py:322
  612.8 8.8 fusion.180
  622.3 5.1 all-to-all-start.16
  627.4 9.0 fusion.178
  636.7 17.0 %add_convert_fusion = bf16[1024,4384]{0,1:T(8,128)(2,1)} fusion(f32[1024,4384]{0,1:T(8,128)} %fusion.180, f32[1024,4384]{0,1:T(8,128)} %fusion.178, pred[]{:T(512)S(6)} %eq.285, bf16[64,32]{1,0:T(8,128)(2,1)S(1)} %copy.587, bf16[64,256]{1,0:T(8,128)(2,1)} %reduce-scatter.10.cloned.1.call-done, bf16[64,2048]{1,0:T(8,128)(2,1)S(1)} %bitcast.1047, ...), kind=kOutput, calls=%fused_computation | convolution fusion | flops 590921728 | bytes 45720064 | tf_op jit(solution)/shard_map/dot_general | solution.py:360
  659.4 9.5 %reduce-scatter.14.cloned.1.call-done = bf16[512,1024]{1,0:T(8,128)(2,1)} async-done(((bf16[2048,1024]{1,0:T(8,128)(2,1)}), bf16[512,1024]{1,0:T(8,128)(2,1)}) %reduce-scatter.14.cloned.1.call-update) | async-done | bytes 1048592 | tf_op jit(solution)/shard_map/reduce_scatter | solution.py:449
  668.9 94.4 %reduce-scatter.12.cloned.1.call-done = bf16[256,4384]{0,1:T(8,128)(2,1)} async-done(((bf16[1024,4384]{0,1:T(8,128)(2,1)}), bf16[256,4384]{0,1:T(8,128)(2,1)}) %reduce-scatter.12.cloned.1.call-update) | async-done | bytes 2244624 | tf_op jit(solution)/shard_map/reduce_scatter | solution.py:446
  764.6 5.5 fusion.157
  770.1 80.2 %all-reduce.27 = (f32[1,1024]{1,0:T(1,128)}, f32[1,4,2304]{2,1,0:T(4,128)}, f32[1,2304]{1,0:T(1,128)}, f32[1,32]{1,0:T(1,128)}, f32[1,32]{1,0:T(1,128)}, /*index=5*/f32[1,32]{1,0:T(1,128)}, f32[1,2048]{1,0:T(1,128)}) all-reduce(f32[1,1024]{1,0:T(1,128)S(1)} %bitcast.1129, ...), channel_id=1, replica_groups=mesh['section'=2,'seq'=4,'wt'=4] {'seq','wt'}, use_global_device_ids=true, to_apply=%region_57.58 | all-reduce | flops 14688 | bytes 117504 | tf_op jit(solution)/shard_map/psum | solution.py:459
  851.3 42.0 %all-reduce.31.cloned.1.call-done = (bf16[1,256,4384]{1,2,0:T(8,128)(2,1)}, bf16[1,512,1024]{2,1,0:T(8,128)(2,1)}) async-done(((bf16[1,256,4384]{1,2,0:T(8,128)(2,1)}, bf16[1,512,1024]{2,1,0:T(8,128)(2,1)}), (bf16[1,256,4384]{1,2,0:T(8,128)(2,1)}, bf16[1,512,1024]{2,1,0:T(8,128)(2,1)})) %all-reduce.31.cloned.1.call-update) | async-done | bytes 3293200 | tf_op jit(solution)/shard_map/psum | solution.py:454
  (1011 shorter events, 300.0 us)
Async XLA Ops:
  7.2 59.4 %copy-start.230 = (f32[1,2304]{1,0:T(1,128)S(1)}, f32[1,2304]{1,0:T(1,128)}, u32[]{:S(2)}) copy-start(f32[1,2304]{1,0:T(1,128)} %param.24) | copy-start | bytes 27652
  7.2 61.9 %slice-start.3 = ((f32[1,2304]{1,0:T(1,128)}), f32[1,256]{1,0:T(1,128)S(1)}, s32[]{:S(2)}) async-start(f32[1,2304]{1,0:T(1,128)} %param.24), calls=%async_computation.34 | async-start | bytes 2048 | tf_op jit(solution)/shard_map/slice | solution.py:241
  7.2 97.8 %all-gather.5.cloned.1.call-start = ((), (), s32[]{:S(2)}) async-start(), calls=%async_computation.28 | async-start | bytes 11223040 | tf_op jit(solution)/shard_map/all_gather | solution.py:391
  8.0 86.1 %copy-start.255 = (f32[1,32]{1,0:T(1,128)S(1)}, f32[1,32]{1,0:T(1,128)}, u32[]{:S(2)}) copy-start(f32[1,32]{1,0:T(1,128)} %param.26) | copy-start | bytes 388
  8.0 97.0 %copy-start.45 = (f32[1,1024]{1,0:T(1,128)S(1)}, f32[1,1024]{1,0:T(1,128)}, u32[]{:S(2)}) copy-start(f32[1,1024]{1,0:T(1,128)} %param.21) | copy-start | bytes 12292
  8.0 167.8 %all-gather.7.cloned.1.call-start = ((), (), s32[]{:S(2)}) async-start(), calls=%async_computation.29 | async-start | bytes 5242880 | tf_op jit(solution)/shard_map/all_gather | solution.py:392
  69.1 151.3 %copy-start.106 = (f32[768]{0:T(1024)}, f32[768]{0:T(1024)S(1)}, u32[]{:S(2)}) copy-start(f32[768]{0:T(1024)S(1)} %pad_maximum_fusion.13) | copy-start | bytes 9220
  111.5 63.7 %copy-start.5 = (f32[64,4384]{1,0:T(8,128)}, f32[64,4384]{1,0:T(8,128)S(1)}, u32[]{:S(2)}) copy-start(f32[64,4384]{1,0:T(8,128)S(1)} %get-tuple-element.381) | copy-start | bytes 3366916
  112.4 19.3 %all-to-all-start.1 = ((bf16[4,2,256]{2,1,0:T(2,128)(2,1)}), bf16[4,2,256]{2,1,0:T(2,128)(2,1)S(1)}, u32[]{:S(2)}, u32[]{:S(2)}) async-start(bf16[4,2,256]{2,1,0:T(2,128)(2,1)} %reshape.3821), calls=%async_computation.1 | async-start | bytes 8192 | tf_op jit(solution)/shard_map/all_to_all | solution.py:290
  131.8 11.3 %all-to-all-start = ((bf16[64,4,512]{2,0,1:T(8,128)(2,1)}), bf16[64,4,512]{2,0,1:T(8,128)(2,1)S(1)}, u32[]{:S(2)}, u32[]{:S(2)}) async-start(bf16[64,4,512]{2,0,1:T(8,128)(2,1)} %bitcast.1002), calls=%async_computation | async-start | bytes 524288 | tf_op jit(solution)/shard_map/all_to_all | solution.py:289
  149.8 25.3 %all-to-all-start.2 = ((bf16[4,64,512]{2,1,0:T(8,128)(2,1)}), bf16[4,64,512]{2,1,0:T(8,128)(2,1)S(1)}, u32[]{:S(2)}, u32[]{:S(2)}) async-start(bf16[4,64,512]{2,1,0:T(8,128)(2,1)} %copy.617), calls=%async_computation.2 | async-start | bytes 524288 | tf_op jit(solution)/shard_map/all_to_all | solution.py:295
  175.8 84.9 %copy-start.32 = (bf16[64,2048]{1,0:T(8,128)(2,1)}, bf16[64,2048]{1,0:T(8,128)(2,1)S(1)}, u32[]{:S(2)}) copy-start(bf16[64,2048]{1,0:T(8,128)(2,1)S(1)} %multiply_convert_fusion.31) | copy-start | bytes 786436
  179.0 2.5 collective-permute-start
  181.6 75.1 %copy-start.12 = (bf16[64,1024]{1,0:T(8,128)(2,1)}, bf16[64,1024]{1,0:T(8,128)(2,1)S(1)}, u32[]{:S(2)}) copy-start(bf16[64,1024]{1,0:T(8,128)(2,1)S(1)} %get-tuple-element.251) | copy-start | bytes 393220
  189.0 19.9 %all-to-all-start.4 = ((bf16[4,2,256]{2,1,0:T(2,128)(2,1)}), bf16[4,2,256]{2,1,0:T(2,128)(2,1)S(1)}, u32[]{:S(2)}, u32[]{:S(2)}) async-start(bf16[4,2,256]{2,1,0:T(2,128)(2,1)} %reshape.3823), calls=%async_computation.4 | async-start | bytes 8192 | tf_op jit(solution)/shard_map/all_to_all | solution.py:290
  208.9 11.5 %all-to-all-start.3 = ((bf16[64,4,512]{2,0,1:T(8,128)(2,1)}), bf16[64,4,512]{2,0,1:T(8,128)(2,1)S(1)}, u32[]{:S(2)}, u32[]{:S(2)}) async-start(bf16[64,4,512]{2,0,1:T(8,128)(2,1)} %bitcast.1001), calls=%async_computation.3 | async-start | bytes 524288 | tf_op jit(solution)/shard_map/all_to_all | solution.py:289
  229.8 26.2 %all-to-all-start.5 = ((bf16[4,64,512]{2,1,0:T(8,128)(2,1)}), bf16[4,64,512]{2,1,0:T(8,128)(2,1)S(1)}, u32[]{:S(2)}, u32[]{:S(2)}) async-start(bf16[4,64,512]{2,1,0:T(8,128)(2,1)} %copy.618), calls=%async_computation.5 | async-start | bytes 524288 | tf_op jit(solution)/shard_map/all_to_all | solution.py:295
  259.1 6.1 collective-permute-start.1
  269.8 20.5 %all-to-all-start.7 = ((bf16[4,2,256]{2,1,0:T(2,128)(2,1)}), bf16[4,2,256]{2,1,0:T(2,128)(2,1)S(1)}, u32[]{:S(2)}, u32[]{:S(2)}) async-start(bf16[4,2,256]{2,1,0:T(2,128)(2,1)} %reshape.3825), calls=%async_computation.7 | async-start | bytes 8192 | tf_op jit(solution)/shard_map/all_to_all | solution.py:290
  290.3 27.6 %all-to-all-start.6 = ((bf16[64,4,512]{2,0,1:T(8,128)(2,1)}), bf16[64,4,512]{2,0,1:T(8,128)(2,1)}, u32[]{:S(2)}, u32[]{:S(2)}) async-start(bf16[64,4,512]{2,0,1:T(8,128)(2,1)} %bitcast.1000), calls=%async_computation.6 | async-start | bytes 524288 | tf_op jit(solution)/shard_map/all_to_all | solution.py:289
  345.1 17.5 %all-to-all-start.8 = ((bf16[4,64,512]{2,1,0:T(8,128)(2,1)}), bf16[4,64,512]{2,1,0:T(8,128)(2,1)}, u32[]{:S(2)}, u32[]{:S(2)}) async-start(bf16[4,64,512]{2,1,0:T(8,128)(2,1)} %copy.619), calls=%async_computation.8 | async-start | bytes 524288 | tf_op jit(solution)/shard_map/all_to_all | solution.py:295
  370.9 12.4 %all-to-all-start.9 = ((bf16[64,4,512]{2,0,1:T(8,128)(2,1)}), bf16[64,4,512]{2,0,1:T(8,128)(2,1)}, u32[]{:S(2)}, u32[]{:S(2)}) async-start(bf16[64,4,512]{2,0,1:T(8,128)(2,1)} %bitcast.1086), calls=%async_computation.9 | async-start | bytes 524288 | tf_op jit(solution)/shard_map/all_to_all | solution.py:339
  417.9 11.3 %all-to-all-start.11 = ((bf16[4,2,256]{2,1,0:T(2,128)(2,1)}), bf16[4,2,256]{2,1,0:T(2,128)(2,1)}, u32[]{:S(2)}, u32[]{:S(2)}) async-start(bf16[4,2,256]{2,1,0:T(2,128)(2,1)} %reshape.3827), calls=%async_computation.12 | async-start | bytes 8192 | tf_op jit(solution)/shard_map/all_to_all | solution.py:352
  421.7 28.7 %reduce-scatter.6.cloned.1.call-start = ((), (), s32[]{:S(2)}) async-start(), calls=%async_computation.23 | async-start | bytes 163840 | tf_op jit(solution)/shard_map/reduce_scatter | solution.py:356
  429.3 19.5 %all-to-all-start.10 = ((bf16[4,64,512]{2,1,0:T(8,128)(2,1)}), bf16[4,64,512]{2,1,0:T(8,128)(2,1)}, u32[]{:S(2)}, u32[]{:S(2)}) async-start(bf16[4,64,512]{2,1,0:T(8,128)(2,1)} %bitcast.1083), calls=%async_computation.10 | async-start | bytes 524288 | tf_op jit(solution)/shard_map/all_to_all | solution.py:345
  457.5 5.9 collective-permute-start.2
  470.9 14.1 %all-to-all-start.12 = ((bf16[64,4,512]{2,0,1:T(8,128)(2,1)}), bf16[64,4,512]{2,0,1:T(8,128)(2,1)}, u32[]{:S(2)}, u32[]{:S(2)}) async-start(bf16[64,4,512]{2,0,1:T(8,128)(2,1)} %bitcast.1087), calls=%async_computation.13 | async-start | bytes 524288 | tf_op jit(solution)/shard_map/all_to_all | solution.py:339
  519.7 10.2 %all-to-all-start.14 = ((bf16[4,2,256]{2,1,0:T(2,128)(2,1)}), bf16[4,2,256]{2,1,0:T(2,128)(2,1)}, u32[]{:S(2)}, u32[]{:S(2)}) async-start(bf16[4,2,256]{2,1,0:T(2,128)(2,1)} %reshape.3829), calls=%async_computation.16 | async-start | bytes 8192 | tf_op jit(solution)/shard_map/all_to_all | solution.py:352
  523.6 26.7 %reduce-scatter.8.cloned.1.call-start = ((), (), s32[]{:S(2)}) async-start(), calls=%async_computation.24 | async-start | bytes 163840 | tf_op jit(solution)/shard_map/reduce_scatter | solution.py:356
  529.9 16.6 %all-to-all-start.13 = ((bf16[4,64,512]{2,1,0:T(8,128)(2,1)}), bf16[4,64,512]{2,1,0:T(8,128)(2,1)}, u32[]{:S(2)}, u32[]{:S(2)}) async-start(bf16[4,64,512]{2,1,0:T(8,128)(2,1)} %bitcast.1084), calls=%async_computation.14 | async-start | bytes 524288 | tf_op jit(solution)/shard_map/all_to_all | solution.py:345
  558.5 3.2 collective-permute-start.3
  565.8 13.1 %all-to-all-start.15 = ((bf16[64,4,512]{2,0,1:T(8,128)(2,1)}), bf16[64,4,512]{2,0,1:T(8,128)(2,1)S(1)}, u32[]{:S(2)}, u32[]{:S(2)}) async-start(bf16[64,4,512]{2,0,1:T(8,128)(2,1)} %bitcast.997), calls=%async_computation.17 | async-start | bytes 524288 | tf_op jit(solution)/shard_map/all_to_all | solution.py:339
  569.2 67.4 %reduce-scatter.10.cloned.1.call-start = ((), (), s32[]{:S(2)}) async-start(), calls=%async_computation.25 | async-start | bytes 163840 | tf_op jit(solution)/shard_map/reduce_scatter | solution.py:356
  595.9 73.0 %reduce-scatter.14.cloned.1.call-start = ((), (), s32[]{:S(2)}) async-start(), calls=%async_computation.27 | async-start | bytes 5242880 | tf_op jit(solution)/shard_map/reduce_scatter | solution.py:449
  609.1 13.1 %all-to-all-start.17 = ((bf16[4,2,256]{2,1,0:T(2,128)(2,1)}), bf16[4,2,256]{2,1,0:T(2,128)(2,1)S(1)}, u32[]{:S(2)}, u32[]{:S(2)}) async-start(bf16[4,2,256]{2,1,0:T(2,128)(2,1)} %reshape.3831), calls=%async_computation.20 | async-start | bytes 8192 | tf_op jit(solution)/shard_map/all_to_all | solution.py:352
  622.3 14.4 %all-to-all-start.16 = ((bf16[4,64,512]{2,1,0:T(8,128)(2,1)}), bf16[4,64,512]{2,1,0:T(8,128)(2,1)S(1)}, u32[]{:S(2)}, u32[]{:S(2)}) async-start(bf16[4,64,512]{2,1,0:T(8,128)(2,1)} %bitcast.282), calls=%async_computation.18 | async-start | bytes 524288 | tf_op jit(solution)/shard_map/all_to_all | solution.py:345
  627.3 135.9 %reduce-scatter.12.cloned.1.call-start = ((), (), s32[]{:S(2)}) async-start(), calls=%async_computation.26 | async-start | bytes 11223040 | tf_op jit(solution)/shard_map/reduce_scatter | solution.py:446
  653.8 239.5 %all-reduce.31.cloned.1.call-start = ((), (), s32[]{:S(2)}) async-start(), calls=%async_computation.30 | async-start | bytes 6586368 | tf_op jit(solution)/shard_map/psum | solution.py:454
  658.4 105.0 %copy-start.177 = (f32[768]{0:T(1024)S(1)}, f32[768]{0:T(1024)}, u32[]{:S(2)}) copy-start(f32[768]{0:T(1024)} %get-tuple-element.186) | copy-start | bytes 9220
  658.4 105.0 %copy-start.176 = (f32[768]{0:T(1024)S(1)}, f32[768]{0:T(1024)}, u32[]{:S(2)}) copy-start(f32[768]{0:T(1024)} %get-tuple-element.262) | copy-start | bytes 9220
  658.5 105.0 %copy-start.175 = (f32[768]{0:T(1024)S(1)}, f32[768]{0:T(1024)}, u32[]{:S(2)}) copy-start(f32[768]{0:T(1024)} %get-tuple-element.264) | copy-start | bytes 9220
  658.5 105.3 %copy-start.131 = (f32[1,8,256]{2,1,0:T(8,128)S(1)}, f32[1,8,256]{2,1,0:T(8,128)}, u32[]{:S(2)}) copy-start(f32[1,8,256]{2,1,0:T(8,128)} %copy-done.130) | copy-start | bytes 24580
  658.5 105.3 %copy-start.133 = (f32[1,8,256]{2,1,0:T(8,128)S(1)}, f32[1,8,256]{2,1,0:T(8,128)}, u32[]{:S(2)}) copy-start(f32[1,8,256]{2,1,0:T(8,128)} %copy-done.132) | copy-start | bytes 24580
  658.5 105.6 %copy-start.256 = (f32[1,32]{1,0:T(1,128)S(1)}, f32[1,32]{1,0:T(1,128)}, u32[]{:S(2)}) copy-start(f32[1,32]{1,0:T(1,128)} %param.26) | copy-start | bytes 388
  658.5 106.1 %copy-start.116 = (bf16[64,256]{1,0:T(8,128)(2,1)S(1)}, bf16[64,256]{1,0:T(8,128)(2,1)}, u32[]{:S(2)}) copy-start(bf16[64,256]{1,0:T(8,128)(2,1)} %reduce-scatter.10.cloned.1.call-done) | copy-start | bytes 98308
  658.5 106.1 %copy-start.215 = (f32[64]{0:T(128)S(1)}, f32[64]{0:T(128)}, u32[]{:S(2)}) copy-start(f32[64]{0:T(128)} %get-tuple-element.364) | copy-start | bytes 772
  764.6 85.7 %copy-start.62 = (f32[64,1024]{1,0:T(8,128)S(1)}, f32[64,1024]{1,0:T(8,128)}, u32[]{:S(2)}) copy-start(f32[64,1024]{1,0:T(8,128)} %copy-done.61) | copy-start | bytes 786436
  764.6 85.8 %copy-start.90 = (f32[1,64,1024]{2,1,0:T(8,128)S(1)}, f32[1,64,1024]{2,1,0:T(8,128)}, u32[]{:S(2)}) copy-start(f32[1,64,1024]{2,1,0:T(8,128)} %get-tuple-element.200) | copy-start | bytes 786436
  (249 other events, 1790.9 us)
Sparse Core Ops, SparseCore 0:
  9.9 95.0 all-gather.4
  106.9 52.6 all-gather.6
  429.4 19.5 reduce-scatter.5
  530.0 20.1 reduce-scatter.7
  596.0 18.1 reduce-scatter.9
  617.9 50.8 reduce-scatter.13
  672.0 91.2 reduce-scatter.11
  765.7 127.4 all-reduce.30
where the time goes:
time: 919 us; the launch traced here: 906 us
  other arithmetic  188 us (20%)
  waiting for transfers between devices  186 us (20%)
  matrix products  158 us (17%)
  blocking collectives  138 us (15%)
  local copies, waits for them, and re-layouts  130 us (14%)
  starting transfers between devices  87.6 us (10%)
  between operations  18.3 us (2%)
    reduce_scatter x1, waiting for transfers between devices, body(): lax.psum_scatter(sum_in.astype(jnp.bfloat16), 'wt', scatter_dimension=0,...  94.4 us
    psum x1, blocking collectives, body(): lax.psum((grad_gain, grad_gate, weight_full, bias_full, step_full, rate_f...  80.2 us
    all_gather x3, blocking collectives, forward_tick(): bc_full = lax.all_gather(sent[:, DI:DI + 2 * N], 'seq', axis=0, tiled=True)  42.6 us
    eq x2, other arithmetic, block_tables(): at_end = starts == starts[:, -1:]  42.3 us
    psum x1, waiting for transfers between devices, body(): lax.psum(shard_in.astype(jnp.bfloat16), 'seq').astype(jnp.float32)  42 us
    sub x5, other arithmetic, mixer_parts(): tables = block_tables(lax.iota(jnp.int32, length) - places)  40.2 us
    dot_general x3, matrix products, backward_tick(): lax.dot_general(normed, grad_proj, CONTRACT_ROWS, preferred_element_type=...  34.8 us
    eq x1, other arithmetic, block_tables(): at_start = starts == starts[:, :1]  22.1 us
  transfers between devices with their start and end apart: 30, of which 12 were waited for; matrix products, arithmetic and copies ran while one was open for 32% of the time, Pallas kernels for 0%

commit v1 on v0

--- a/solution.py
+++ b/solution.py
@@ -1,6 +1,10 @@
+import functools
+
 import jax
 import jax.numpy as jnp
 from jax import lax
+from jax.experimental import pallas as pl
+from jax.experimental.pallas import tpu as pltpu
 from jax.sharding import PartitionSpec as P
 
 H = 32
@@ -246,131 +250,197 @@
     return (columns, biases, step_bias, rates, skips)
 
 
-def place_heads(head_grads):
-    grad_columns, grad_biases, grad_step_bias, grad_rate_log, grad_skip = head_grads
-    width = grad_step_bias.shape[0]
-    first = lax.axis_index("seq") * width
-    weight_full = jnp.concatenate(
-        [
-            lax.dynamic_update_slice_in_dim(
-                jnp.zeros((K, DI), jnp.float32),
-                grad_columns[:, : width * P_SIZE],
-                first * P_SIZE,
-                1,
-            ),
-            grad_columns[:, width * P_SIZE :],
+def exchange_kernel(size, spread, src, dst, send, recv, here):
+    me = lax.axis_index("seq")
+    barrier = pltpu.get_barrier_semaphore()
+    for distance in range(1, size):
+        pl.semaphore_signal(
+            barrier,
+            inc=1,
+            device_id={"seq": lax.rem(me + distance, size)},
+            device_id_type=pl.DeviceIdType.MESH,
+        )
+    own = pltpu.make_async_copy(src if spread else src.at[me], dst.at[me], here)
+    own.start()
+    pl.semaphore_wait(barrier, size - 1)
+    copies = []
+    for distance in range(1, size):
+        peer = lax.rem(me + distance, size)
+        copy = pltpu.make_async_remote_copy(
+            src_ref=src if spread else src.at[peer],
+            dst_ref=dst.at[me],
+            send_sem=send.at[distance - 1],
+            recv_sem=recv.at[distance - 1],
+            device_id={"seq": peer},
+            device_id_type=pl.DeviceIdType.MESH,
+        )
+        copy.start()
+        copies.append(copy)
+    own.wait()
+    for copy in copies:
+        copy.wait()
+
+
+def exchange(block, spread, call_id):
+    size = lax.axis_size("seq")
+    part = block.shape if spread else block.shape[1:]
+    return pl.pallas_call(
+        functools.partial(exchange_kernel, size, spread),
+        out_shape=jax.ShapeDtypeStruct((size,) + part, block.dtype),
+        in_specs=[pl.BlockSpec(memory_space=pltpu.VMEM)],
+        out_specs=pl.BlockSpec(memory_space=pltpu.VMEM),
+        scratch_shapes=[
+            pltpu.SemaphoreType.DMA((size - 1,)),
+            pltpu.SemaphoreType.DMA((size - 1,)),
+            pltpu.SemaphoreType.DMA,
         ],
-        1,
-    )
-    bias_full = jnp.concatenate(
-        [
-            lax.dynamic_update_slice_in_dim(
-                jnp.zeros((DI,), jnp.float32), grad_biases[: width * P_SIZE], first * P_SIZE, 0
-            ),
-            grad_biases[width * P_SIZE :],
-        ],
-        0,
-    )
-    spread_out = [
-        lax.dynamic_update_slice_in_dim(jnp.zeros((H,), jnp.float32), member, first, 0)
-        for member in (grad_step_bias, grad_rate_log, grad_skip)
-    ]
-    return (weight_full, bias_full, spread_out[0], spread_out[1], spread_out[2])
-
-
-def forward_tick(inputs, places, w_in, w_out, gain, gate, heads):
+        compiler_params=pltpu.CompilerParams(
+            collective_id=call_id, has_side_effects=True, vmem_limit_bytes=48 * 1024 * 1024
+        ),
+    )(block)
+
+
+def gather_seq(block, call_id):
+    return exchange(block, True, call_id).reshape((-1,) + block.shape[1:])
+
+
+def swap_seq(block, call_id):
+    size = lax.axis_size("seq")
+    rows = block.shape[0] // size
+    return exchange(block.reshape((size, rows) + block.shape[1:]), False, call_id)
+
+
+SIDE = 128
+
+
+def side_columns(values):
+    columns = []
+    for value in values:
+        for _ in range(3):
+            term = value.astype(jnp.bfloat16)
+            columns.append(term)
+            value = value - term.astype(jnp.float32)
+    stacked = jnp.stack(columns, axis=1)
+    return jnp.pad(stacked, ((0, 0), (0, SIDE - stacked.shape[1])))
+
+
+def side_value(columns, index):
+    return jnp.sum(columns[..., 3 * index : 3 * index + 3].astype(jnp.float32), axis=-1)
+
+
+def input_norm(inputs, gain):
     section_in = inputs.astype(jnp.float32)
     scale = lax.rsqrt(jnp.mean(section_in * section_in, axis=-1, keepdims=True) + EPSILON)
-    normed = (section_in * scale * gain).astype(jnp.bfloat16)
+    return (section_in, scale, (section_in * scale * gain).astype(jnp.bfloat16))
+
+
+def forward_tick(inputs, places, w_in, w_out, gain, gate, heads):
+    inner = w_out.shape[0]
+    width = inner // P_SIZE
+    normed = input_norm(gather_seq(inputs, 0), gain)[2]
     proj = jnp.dot(normed, w_in, preferred_element_type=jnp.float32)
-    z_gate = proj[:, :DI]
-    sent = proj[:, DI:].astype(jnp.bfloat16)
-    x_heads, step_raw = (
-        lax.all_to_all(sent[:, :DI], "seq", split_axis=1, concat_axis=0, tiled=True),
-        lax.all_to_all(sent[:, DI + 2 * N :], "seq", split_axis=1, concat_axis=0, tiled=True),
-    )
-    bc_full = lax.all_gather(sent[:, DI : DI + 2 * N], "seq", axis=0, tiled=True)
-    channels = jnp.concatenate([x_heads, bc_full], 1)
-    mixed = mixer_forward(channels, step_raw, places, heads)
-    y_tok = lax.all_to_all(
-        mixed.astype(jnp.bfloat16), "seq", split_axis=0, concat_axis=1, tiled=True
-    )
-    gated = y_tok.astype(jnp.float32) * jax.nn.silu(z_gate)
-    gate_scale = lax.rsqrt(jnp.mean(gated * gated, axis=-1, keepdims=True) + EPSILON)
-    normed_out = (gated * gate_scale * gate).astype(jnp.bfloat16)
-    result = (section_in + jnp.dot(normed_out, w_out, preferred_element_type=jnp.float32)).astype(
-        jnp.bfloat16
-    )
-    kept = (
-        inputs,
-        scale,
-        normed,
-        z_gate,
-        channels,
-        step_raw,
-        y_tok,
-        gate_scale,
-        normed_out,
-        places,
-    )
-    return (result, kept)
+    z_gate = proj[:, :inner]
+    channels = proj[:, inner : 2 * inner + 2 * N].astype(jnp.bfloat16)
+    step_raw = proj[:, 2 * inner + 2 * N : 2 * inner + 2 * N + width].astype(jnp.bfloat16)
+    y_row = mixer_forward(channels, step_raw, places, heads).astype(jnp.bfloat16)
+    gated = y_row.astype(jnp.float32) * jax.nn.silu(z_gate)
+    part = jnp.dot((gated * gate).astype(jnp.bfloat16), w_out, preferred_element_type=jnp.float32)
+    power = jnp.sum(gated * gated, axis=-1)
+    parts = swap_seq(
+        jnp.concatenate([part.astype(jnp.bfloat16), side_columns([power])], 1), 1
+    )
+    features = inputs.shape[1]
+    power = jnp.sum(side_value(parts[:, :, features:], 0), axis=0)
+    gate_scale = lax.rsqrt(power / DI + EPSILON)
+    branch = jnp.sum(parts[:, :, :features].astype(jnp.float32), axis=0) * gate_scale[:, None]
+    result = (inputs.astype(jnp.float32) + branch).astype(jnp.bfloat16)
+    return (result, (inputs, normed, z_gate, channels, step_raw, y_row, gate_scale, branch, places))
 
 
 def backward_tick(grad_out, kept, w_in, w_out, gain, gate, heads):
-    inputs, scale, normed, z_gate, channels, step_raw, y_tok, gate_scale, normed_out, places = kept
+    inputs, normed, z_gate, channels, step_raw, y_row, gate_scale, branch, places = kept
+    features = inputs.shape[1]
     grad_low = grad_out.astype(jnp.bfloat16)
-    grad_w_out = lax.dot_general(
-        normed_out, grad_low, CONTRACT_ROWS, preferred_element_type=jnp.float32
-    )
+    along = jnp.sum(grad_low.astype(jnp.float32) * branch, axis=-1)
+    row = gather_seq(jnp.concatenate([grad_low, side_columns([gate_scale, along])], 1), 2)
+    grad_row = row[:, :features]
+    row_scale = side_value(row[:, features:], 0)[:, None]
+    row_along = side_value(row[:, features:], 1)[:, None]
     grad_normed_out = lax.dot_general(
-        grad_low, w_out, CONTRACT_COLS, preferred_element_type=jnp.float32
-    )
-    y_float = y_tok.astype(jnp.float32)
+        grad_row, w_out, CONTRACT_COLS, preferred_element_type=jnp.float32
+    )
+    y_float = y_row.astype(jnp.float32)
     z_swish = jax.nn.silu(z_gate)
     gated = y_float * z_swish
-    grad_gate = jnp.sum(grad_normed_out * gated * gate_scale, axis=0)
-    scaled_grad = grad_normed_out * gate
-    grad_gated = gate_scale * (
-        scaled_grad
-        - gated * gate_scale * gate_scale * jnp.mean(scaled_grad * gated, axis=-1, keepdims=True)
-    )
+    scaled = gated * row_scale
+    normed_out = (scaled * gate).astype(jnp.bfloat16)
+    grad_gate = jnp.sum(grad_normed_out * scaled, axis=0)
+    grad_gated = row_scale * (grad_normed_out * gate - scaled * (row_along / DI))
     grad_y = (grad_gated * z_swish).astype(jnp.bfloat16)
     grad_z = grad_gated * y_float * swish_slope(z_gate)
-    grad_heads = lax.all_to_all(grad_y, "seq", split_axis=1, concat_axis=0, tiled=True)
     grad_chan, grad_step_raw, head_grads = mixer_backward(
-        grad_heads, channels, step_raw, places, heads
-    )
-    width = step_raw.shape[1]
-    back_x, back_step = (
-        lax.all_to_all(
-            grad_chan[:, : width * P_SIZE].astype(jnp.bfloat16),
-            "seq",
-            split_axis=0,
-            concat_axis=1,
-            tiled=True,
-        ),
-        lax.all_to_all(
-            grad_step_raw.astype(jnp.bfloat16), "seq", split_axis=0, concat_axis=1, tiled=True
-        ),
-    )
-    back_bc = lax.psum_scatter(
-        grad_chan[:, width * P_SIZE :].astype(jnp.bfloat16), "seq", scatter_dimension=0, tiled=True
-    )
-    grad_proj = jnp.concatenate([grad_z.astype(jnp.bfloat16), back_x, back_bc, back_step], 1)
-    grad_w_in = lax.dot_general(
-        normed, grad_proj, CONTRACT_ROWS, preferred_element_type=jnp.float32
-    )
-    grad_normed = lax.dot_general(
-        grad_proj, w_in, CONTRACT_COLS, preferred_element_type=jnp.float32
-    )
-    section_in = inputs.astype(jnp.float32)
+        grad_y, channels, step_raw, places, heads
+    )
+    grad_proj = jnp.concatenate([grad_z, grad_chan, grad_step_raw], 1).astype(jnp.bfloat16)
+    grad_proj = jnp.pad(grad_proj, ((0, 0), (0, w_in.shape[1] - grad_proj.shape[1])))
+    part = lax.dot_general(grad_proj, w_in, CONTRACT_COLS, preferred_element_type=jnp.float32)
+    grad_normed = jnp.sum(swap_seq(part.astype(jnp.bfloat16), 3).astype(jnp.float32), axis=0)
+    section_in, scale, _ = input_norm(inputs, gain)
     grad_gain = jnp.sum(grad_normed * section_in * scale, axis=0)
     scaled_in = grad_normed * gain
     grad_in = grad_out + scale * (
         scaled_in
         - section_in * scale * scale * jnp.mean(scaled_in * section_in, axis=-1, keepdims=True)
     )
-    return (grad_in, grad_w_in, grad_w_out, (grad_gain, grad_gate) + head_grads)
+    smalls = (grad_gain, grad_gate) + head_grads
+    return (grad_in, (normed, grad_proj), (normed_out, grad_row), smalls)
+
+
+def group_columns(w_in, inner):
+    me = lax.axis_index("seq")
+    width = inner // P_SIZE
+    parts = [
+        lax.dynamic_slice_in_dim(w_in, me * inner, inner, 1),
+        lax.dynamic_slice_in_dim(w_in, DI + me * inner, inner, 1),
+        w_in[:, 2 * DI : 2 * DI + 2 * N],
+        lax.dynamic_slice_in_dim(w_in, 2 * DI + 2 * N + me * width, width, 1),
+    ]
+    used = 2 * inner + 2 * N + width
+    return jnp.pad(jnp.concatenate(parts, 1), ((0, 0), (0, -used % 128)))
+
+
+def transposed_route(seq, wt):
+    return [(s * wt + w, w * wt + s) for s in range(seq) for w in range(wt)]
+
+
+def sum_small(small_totals):
+    grad_gain, grad_gate, columns, biases, step_bias, rate_log, skip = small_totals
+    me = lax.axis_index("seq")
+    width = step_bias.shape[0]
+    inner = width * P_SIZE
+
+    def placed(member, size):
+        shape = member.shape[:-1] + (size,)
+        return lax.dynamic_update_slice_in_dim(
+            jnp.zeros(shape, jnp.float32), member, me * member.shape[-1], member.ndim - 1
+        )
+
+    grads = [
+        grad_gain,
+        placed(grad_gate, DI),
+        jnp.concatenate([placed(columns[:, :inner], DI), columns[:, inner:]], 1),
+        jnp.concatenate([placed(biases[:inner], DI), biases[inner:]], 0),
+        placed(step_bias, H),
+        placed(rate_log, H),
+        placed(skip, H),
+    ]
+    flat = lax.psum(jnp.concatenate([g.reshape(-1) for g in grads]), ("seq", "wt"))
+    summed = []
+    first = 0
+    for grad in grads:
+        summed.append(flat[first : first + grad.size].reshape(grad.shape))
+        first += grad.size
+    return summed
 
 
 def body(
@@ -387,13 +457,20 @@
     gate_gain,
     out_weight,
 ):
-    w_in, w_out = (
-        lax.all_gather(in_weight[0], "wt", axis=0, tiled=True),
-        lax.all_gather(out_weight[0], "wt", axis=0, tiled=True),
-    )
+    seq, wt = (lax.axis_size("seq"), lax.axis_size("wt"))
+    me = lax.axis_index("seq")
+    width = H // seq
+    inner = width * P_SIZE
+    w_in = lax.all_gather(group_columns(in_weight[0], inner), "wt", axis=0, tiled=True)
+    if seq == wt:
+        w_out = lax.ppermute(out_weight[0], ("seq", "wt"), transposed_route(seq, wt))
+    else:
+        w_out = lax.dynamic_slice_in_dim(
+            lax.all_gather(out_weight[0], "wt", axis=0, tiled=True), me * inner, inner, 0
+        )
     places_all = lax.all_gather(positions, "seq", axis=2, tiled=True)
     gain = norm_gain[0]
-    gate = gate_gain[0]
+    gate = lax.dynamic_slice_in_dim(gate_gain[0], me * inner, inner, 0)
     heads = head_params(conv_weight[0], conv_bias[0], dt_bias[0], a_log[0], skip_d[0])
     first_section = lax.axis_index("section") == 0
     batches = block_input.shape[0]
@@ -415,8 +492,8 @@
             received = from_behind(result, "section", 1)
     grad_recv = jnp.zeros(block_input.shape[2:], jnp.float32)
     grad_ticks = []
-    sum_in = jnp.zeros(w_in.shape, jnp.float32)
-    sum_out = jnp.zeros(w_out.shape, jnp.float32)
+    in_ticks = []
+    out_pairs = []
     small_totals = None
     for step_index in range(batches + 1):
         if step_index < batches:
@@ -429,12 +506,12 @@
             kept_ticks[max(step_index - 1, 0)],
             kept_ticks[min(step_index + 1, batches)],
         )
-        grad_in, grad_w_in, grad_w_out, smalls = backward_tick(
+        grad_in, in_pair, out_pair, smalls = backward_tick(
             grad_out, chosen, w_in, w_out, gain, gate, heads
         )
         grad_ticks.append(grad_in)
-        sum_in = sum_in + grad_w_in
-        sum_out = sum_out + grad_w_out
+        in_ticks.append(in_pair)
+        out_pairs.append(out_pair)
         small_totals = (
             smalls if small_totals is None else jax.tree.map(jnp.add, small_totals, smalls)
         )
@@ -442,24 +519,51 @@
             grad_recv = from_behind(grad_in.astype(jnp.bfloat16), "section", -1).astype(
                 grad_in.dtype
             )
-    shard_in, shard_out = (
-        lax.psum_scatter(sum_in.astype(jnp.bfloat16), "wt", scatter_dimension=0, tiled=True).astype(
-            jnp.float32
-        ),
-        lax.psum_scatter(
-            sum_out.astype(jnp.bfloat16), "wt", scatter_dimension=0, tiled=True
-        ).astype(jnp.float32),
-    )
-    total_in, total_out = (
-        lax.psum(shard_in.astype(jnp.bfloat16), "seq").astype(jnp.float32),
-        lax.psum(shard_out.astype(jnp.bfloat16), "seq").astype(jnp.float32),
-    )
-    grad_gain, grad_gate = (small_totals[0], small_totals[1])
-    weight_full, bias_full, step_full, rate_full, skip_full = place_heads(small_totals[2:])
-    summed = lax.psum(
-        (grad_gain, grad_gate, weight_full, bias_full, step_full, rate_full, skip_full),
-        ("seq", "wt"),
-    )
+
+    def all_tokens(pairs, which):
+        return jnp.concatenate(
+            [
+                jnp.where(first_section, pairs[index + 1][which], pairs[index][which])
+                for index in range(batches)
+            ]
+        )
+
+    def weight_grad(pairs):
+        return lax.dot_general(
+            all_tokens(pairs, 0),
+            all_tokens(pairs, 1),
+            CONTRACT_ROWS,
+            preferred_element_type=jnp.float32,
+        ).astype(jnp.bfloat16)
+
+    grad_out_group = weight_grad(out_pairs)
+    if seq == wt:
+        total_out = lax.ppermute(
+            lax.psum(grad_out_group, "wt"), ("seq", "wt"), transposed_route(seq, wt)
+        )
+    else:
+        placed_out = lax.dynamic_update_slice_in_dim(
+            jnp.zeros((DI, grad_out_group.shape[1]), jnp.bfloat16), grad_out_group, me * inner, 0
+        )
+        total_out = lax.psum(
+            lax.psum_scatter(placed_out, "wt", scatter_dimension=0, tiled=True), "seq"
+        )
+    total_out = total_out.astype(jnp.float32)
+    shard_in = lax.psum_scatter(weight_grad(in_ticks), "wt", scatter_dimension=0, tiled=True)
+    groups = lax.all_gather(shard_in, "seq", axis=0)
+    ends = 2 * inner + 2 * N
+    total_in = jnp.concatenate(
+        [groups[index, :, :inner] for index in range(seq)]
+        + [groups[index, :, inner : 2 * inner] for index in range(seq)]
+        + [
+            jnp.sum(groups[:, :, 2 * inner : ends].astype(jnp.float32), axis=0).astype(
+                jnp.bfloat16
+            )
+        ]
+        + [groups[index, :, ends : ends + width] for index in range(seq)],
+        1,
+    ).astype(jnp.float32)
+    summed = sum_small(small_totals)
     section_rows = jnp.stack(
         [
             jnp.where(first_section, out_ticks[index], out_ticks[index + 1])

time: 919 us -> 887 us (0.965)
  Pallas kernels: 0 us -> 236 us
  waiting for transfers between devices: 186 us -> 68.1 us
  matrix products: 158 us -> 68.1 us
  starting transfers between devices: 87.6 us -> 10.1 us
  local copies, waits for them, and re-layouts: 130 us -> 56.8 us
  blocking collectives: 138 us -> 192 us
  other arithmetic: 188 us -> 226 us
    pallas_call x0 -> x12, Pallas kernels: none -> 236 us  [exchange(): pl.pallas_call(functools.partial(exchange_kernel, size, spread), out_shap...]
    psum x1, blocking collectives: 80.2 us -> 179 us  [sum_small(): lax.psum(jnp.concatenate([g.reshape(-1) for g in grads]), ('seq', 'wt'))]
    all_to_all x18 -> x0, starting transfers between devices: 81.6 us -> none  [the longest x3 15.2 us: backward_tick(): lax.all_to_all(grad_chan[:, :width * P_SIZE].astype(jnp.bfloat16), 'seq',...]
    reduce_scatter x5 -> x1, waiting for transfers between devices: 106 us -> 31.4 us  [body(): lax.psum_scatter(weight_grad(in_ticks), 'wt', scatter_dimension=0, tiled=...]
    dot_general x12 -> x8, matrix products: 69.8 us -> 20 us  [the longest x3 10.8 us: backward_tick(): lax.dot_general(grad_row, w_out, CONTRACT_COLS, preferred_element_type=jn...]
    all_gather x3 -> x0, blocking collectives: 42.6 us -> none  [forward_tick(): bc_full = lax.all_gather(sent[:, DI:DI + 2 * N], 'seq', axis=0, tiled=True)]
    convert_element_type x42 -> x0, local copies, waits for them, and re-layouts: 32.6 us -> none  [the longest x9 12.6 us: scan_values(): inflow = (x_blocks * inflow_scale).astype(jnp.bfloat16)]
    all_to_all x18 -> x0, waiting for transfers between devices: 26.3 us -> none  [the longest x3 12.6 us: backward_tick(): lax.all_to_all(grad_y, 'seq', split_axis=1, concat_axis=0, tiled=True)]
  transfers between devices with their start and end apart: 30 -> 10, of which waited for: 12 -> 4; matrix products, arithmetic and copies ran while one was open for 32% -> 18% of each run, Pallas kernels for 0% -> 11%
where the time goes in v1:
time: 887 us; the launch traced here: 875 us
  Pallas kernels  236 us (27%)
  other arithmetic  226 us (25%)
  blocking collectives  192 us (22%)
  waiting for transfers between devices  68.1 us (8%)
  matrix products  68.1 us (8%)
  local copies, waits for them, and re-layouts  56.8 us (6%)
  between operations  18.1 us (2%)
  starting transfers between devices  10.1 us (1%)
    pallas_call x12, Pallas kernels, exchange(): pl.pallas_call(functools.partial(exchange_kernel, size, spread), out_shap...  236 us
    psum x1, blocking collectives, sum_small(): lax.psum(jnp.concatenate([g.reshape(-1) for g in grads]), ('seq', 'wt'))  179 us
    sub x5, other arithmetic, mixer_parts(): tables = block_tables(lax.iota(jnp.int32, length) - places)  37.9 us
    psum x1, waiting for transfers between devices, body(): lax.psum(grad_out_group, 'wt')  34.2 us
    eq x2, other arithmetic, block_tables(): at_start = starts == starts[:, :1]  33.4 us
    eq x2, other arithmetic, block_tables(): at_end = starts == starts[:, -1:]  32.3 us
    reduce_scatter x1, waiting for transfers between devices, body(): lax.psum_scatter(weight_grad(in_ticks), 'wt', scatter_dimension=0, tiled=...  31.4 us
    another operation x36, other arithmetic  18.4 us
  transfers between devices with their start and end apart: 10, of which 4 were waited for; matrix products, arithmetic and copies ran while one was open for 18% of the time, Pallas kernels for 11%

profile of v1, /device:TPU:0, one launch (start us, length us, event | category | flops | bytes accessed | tf_op | source)
XLA Modules:
  0.0 875.1 jit_solution(9298256690692279662)
XLA Ops:
  11.0 2.0 collective-permute-start
  13.1 81.0 %shard_map.203 = bf16[4,64,1024]{2,1,0:T(8,128)(2,1)S(1)} custom-call(bf16[64,1024]{1,0:T(8,128)(2,1)S(1)} %select_bitcast_fusion.2.src), custom_call_target="tpu_custom_call" | custom-call | tf_op jit(solution)/shard_map/pallas_call | solution.py:287
  97.1 13.3 %all_gather.13 = s32[2,1,256]{0,1,2:T(1,128)S(1)} all-gather(s32[2,1,64]{0,1,2:T(1,128)S(1)} %copy.734), channel_id=1, replica_groups=mesh['section'=2,'seq'=4,'wt'=4] {'seq'}, dimensions={2}, use_global_device_ids=true | all-gather | bytes 2560 | tf_op jit(solution)/shard_map/all_gather | solution.py:471
  112.2 4.9 fusion.347
  117.2 33.0 %fusion.352 = (s32[256]{0:T(256)S(1)}, s32[1,1,256]{0,1,2:T(1,128)S(1)}, s32[256]{0:T(256)S(1)}, s32[1,1,256]{0,1,2:T(1,128)S(1)}, s32[256]{0:T(256)S(1)}, /*ind...) fusion(s32[2,1,256]{0,1,2:T(1,128)S(1)} %all_gather.13, pred[]{:T(512)S(6)} %eq.285, ...), kind=kLoop, calls=%fused_computation.826 | loop fusion | flops 1792 | bytes 12289 | tf_op jit(solution)/shard_map/sub | solution.py:128
  152.5 11.0 %compare_reduce_fusion.8 = (pred[256]{0:T(512)(128)(4,1)}, pred[256]{0:T(512)(128)(4,1)}) fusion(s32[]{:T(128)} %bitcast.76, s32[1,1,256]{0,1,2:T(1,128)S(1)} %get-tuple-element.229, s32[]{:T(128)} %bitcast.62), kind=kLoop, calls=%fused_computation.314 | loop fusion | flops 768 | bytes 1544 | tf_op jit(solution)/shard_map/eq | solution.py:74
  163.5 21.3 %compare_reduce_fusion.2 = (pred[256]{0:T(512)(128)(4,1)}, pred[256]{0:T(512)(128)(4,1)}, pred[256]{0:T(512)(128)(4,1)}, pred[256]{0:T(512)(128)(4,1)}) fusion(s32[1,1,256]{0,1,2:T(1,128)S(1)} %get-tuple-element.243, s32[]{:T(128)} %bitcast.214, s32[]{:T(128)} %bitcast.195, s32[1,1,256]{0,1,2:T(1,128)S(1)} %get-tuple-element.350, s32[]{:T(128)} %bitcast.128, ...), kind=kLoop, calls=%fused_computation.308 | loop fusion | flops 1024 | bytes 3088 | tf_op jit(solution)/shard_map/eq | solution.py:73
  184.8 22.4 %compare_reduce_fusion.6 = (pred[256]{0:T(512)(128)(4,1)}, pred[256]{0:T(512)(128)(4,1)S(1)}, pred[256]{0:T(512)(128)(4,1)S(1)}, pred[256]{0:T(512)(128)(4,1)}) fusion(s32[]{:T(128)} %bitcast.111, s32[2,1,256]{0,1,2:T(1,128)S(1)} %all_gather.13, s32[]{:T(128)} %bitcast.38, s32[]{:T(128)} %bitcast.24, s32[]{:T(128)} %bitcast.97), kind=kLoop, calls=%fused_computation.312 | loop fusion | flops 1536 | bytes 3088 | tf_op jit(solution)/shard_map/eq | solution.py:74
  213.0 2.9 fusion.369
  222.6 2.0 fusion.28
  227.9 11.0 %shard_map.204 = bf16[4,64,1152]{2,1,0:T(8,128)(2,1)S(1)} custom-call(bf16[4,64,1152]{2,1,0:T(8,128)(2,1)S(1)} %bitcast.944), custom_call_target="tpu_custom_call" | custom-call | tf_op jit(solution)/shard_map/pallas_call | solution.py:287
  241.8 11.0 %compare_reduce_fusion = (pred[256]{0:T(512)(128)(4,1)}, pred[256]{0:T(512)(128)(4,1)}) fusion(s32[1,1,256]{0,1,2:T(1,128)S(1)} %copy-done.75, s32[]{:T(128)} %bitcast.281, s32[]{:T(128)} %bitcast.262), kind=kLoop, calls=%fused_computation.306 | loop fusion | flops 512 | bytes 1544 | tf_op jit(solution)/shard_map/eq | solution.py:73
  254.2 12.6 %shard_map.205 = bf16[4,64,1024]{2,1,0:T(8,128)(2,1)S(1)} custom-call(bf16[64,1024]{1,0:T(8,128)(2,1)S(1)} %get-tuple-element.254.src), custom_call_target="tpu_custom_call" | custom-call | tf_op jit(solution)/shard_map/pallas_call | solution.py:287
  267.4 3.9 fusion.370
  276.6 2.1 fusion.29
  278.6 2.1 multiply_reduce_fusion.34
  282.7 14.1 %shard_map.206 = bf16[4,64,1152]{2,1,0:T(8,128)(2,1)S(1)} custom-call(bf16[4,64,1152]{2,1,0:T(8,128)(2,1)S(1)} %bitcast.945), custom_call_target="tpu_custom_call" | custom-call | tf_op jit(solution)/shard_map/pallas_call | solution.py:287
  304.1 14.1 %shard_map.207 = bf16[4,64,1024]{2,1,0:T(8,128)(2,1)S(1)} custom-call(bf16[64,1024]{1,0:T(8,128)(2,1)S(1)} %get-tuple-element.221.src), custom_call_target="tpu_custom_call" | custom-call | tf_op jit(solution)/shard_map/pallas_call | solution.py:287
  321.1 2.1 fusion.371
  326.6 2.9 multiply_convert_fusion.12
  333.8 3.1 broadcast_select_fusion.17
  339.0 15.0 %shard_map.208 = bf16[4,64,1152]{2,1,0:T(8,128)(2,1)S(1)} custom-call(bf16[4,64,1152]{2,1,0:T(8,128)(2,1)S(1)} %bitcast.946), custom_call_target="tpu_custom_call" | custom-call | tf_op jit(solution)/shard_map/pallas_call | solution.py:287
  356.9 3.0 multiply_convert_fusion.13
  376.9 16.1 %shard_map.209 = bf16[4,64,1152]{2,1,0:T(8,128)(2,1)S(1)} custom-call(bf16[64,1152]{1,0:T(8,128)(2,1)S(1)} %fusion.187.src), custom_call_target="tpu_custom_call" | custom-call | tf_op jit(solution)/shard_map/pallas_call | solution.py:287
  393.3 3.6 fusion.103
  399.1 2.1 multiply_reduce_fusion.8
  422.7 2.6 fusion.335
  428.4 2.3 multiply_reduce_fusion.29
  433.8 13.4 %shard_map.210 = bf16[4,64,1024]{2,1,0:T(8,128)(2,1)S(1)} custom-call(bf16[4,64,1024]{2,1,0:T(8,128)(2,1)S(1)} %bitcast.948), custom_call_target="tpu_custom_call" | custom-call | tf_op jit(solution)/shard_map/pallas_call | solution.py:287
  452.5 14.9 %shard_map.211 = bf16[4,64,1152]{2,1,0:T(8,128)(2,1)S(1)} custom-call(bf16[64,1152]{1,0:T(8,128)(2,1)S(1)} %fusion.188.src), custom_call_target="tpu_custom_call" | custom-call | tf_op jit(solution)/shard_map/pallas_call | solution.py:287
  467.6 2.5 fusion.174
  470.2 3.5 fusion.110
  476.0 2.0 multiply_reduce_fusion.6
  498.1 2.3 fusion.334
  507.2 13.8 %shard_map.212 = bf16[4,64,1024]{2,1,0:T(8,128)(2,1)S(1)} custom-call(bf16[4,64,1024]{2,1,0:T(8,128)(2,1)S(1)} %bitcast.949), custom_call_target="tpu_custom_call" | custom-call | tf_op jit(solution)/shard_map/pallas_call | solution.py:287
  526.6 16.6 %shard_map.213 = bf16[4,64,1152]{2,1,0:T(8,128)(2,1)S(1)} custom-call(bf16[64,1152]{1,0:T(8,128)(2,1)S(1)} %fusion.189.src), custom_call_target="tpu_custom_call" | custom-call | tf_op jit(solution)/shard_map/pallas_call | solution.py:287
  543.4 2.4 fusion.175
  545.9 3.7 fusion.117
  551.1 2.0 multiply_reduce_fusion.4
  559.6 2.6 fusion.336
  562.2 2.5 multiply_reduce_fusion.17
  569.0 3.4 convolution_convert_fusion
  586.0 31.4 %reduce-scatter.2.cloned.1.call-done = bf16[256,1408]{1,0:T(8,128)(2,1)} async-done(((bf16[1024,1408]{1,0:T(8,128)(2,1)}), bf16[256,1408]{1,0:T(8,128)(2,1)}) %reduce-scatter.2.cloned.1.call-update) | async-done | bytes 720912 | tf_op jit(solution)/shard_map/reduce_scatter | solution.py:552
  622.4 2.1 convolution_convert_fusion.5
  624.7 13.0 %shard_map.214 = bf16[4,64,1024]{2,1,0:T(8,128)(2,1)S(1)} custom-call(bf16[4,64,1024]{2,1,0:T(8,128)(2,1)S(1)} %bitcast.947), custom_call_target="tpu_custom_call" | custom-call | tf_op jit(solution)/shard_map/pallas_call | solution.py:287
  639.5 34.2 %all-reduce.39.cloned.1.call-done = bf16[512,1024]{1,0:T(8,128)(2,1)} async-done(((bf16[512,1024]{1,0:T(8,128)(2,1)}), bf16[512,1024]{1,0:T(8,128)(2,1)}) %all-reduce.39.cloned.1.call-update) | async-done | bytes 1048592 | tf_op jit(solution)/shard_map/psum | solution.py:542
  675.8 178.6 %psum.14 = f32[14688]{0:T(1024)S(1)} all-reduce(f32[14688]{0:T(1024)S(1)} %concatenate.217), channel_id=1, replica_groups=mesh['section'=2,'seq'=4,'wt'=4] {'seq','wt'}, use_global_device_ids=true, to_apply=%region_102.103 | all-reduce | flops 14688 | bytes 117504 | tf_op jit(solution)/shard_map/psum | solution.py:437
  865.6 2.5 convert_element_type.1514
  (930 shorter events, 192.2 us)
Async XLA Ops:
  7.2 103.9 %copy-start = (f32[1,2048]{1,0:T(1,128)S(1)}, f32[1,2048]{1,0:T(1,128)}, u32[]{:S(2)}) copy-start(f32[1,2048]{1,0:T(1,128)} %param.28) | copy-start | bytes 24580
  7.2 205.8 %all-gather.4.cloned.1.call-start = ((), (), s32[]{:S(2)}) async-start(), calls=%async_computation.1 | async-start | bytes 3604480 | tf_op jit(solution)/shard_map/all_gather | solution.py:464
  8.9 86.1 %copy-start.246 = (f32[1,32]{1,0:T(1,128)S(1)}, f32[1,32]{1,0:T(1,128)}, u32[]{:S(2)}) copy-start(f32[1,32]{1,0:T(1,128)} %param.26) | copy-start | bytes 388
  8.9 86.1 %copy-start.252 = (f32[1,32]{1,0:T(1,128)S(1)}, f32[1,32]{1,0:T(1,128)}, u32[]{:S(2)}) copy-start(f32[1,32]{1,0:T(1,128)} %param.27) | copy-start | bytes 388
  8.9 86.7 %copy-start.262 = (f32[1,32]{1,0:T(1,128)S(1)}, f32[1,32]{1,0:T(1,128)}, u32[]{:S(2)}) copy-start(f32[1,32]{1,0:T(1,128)} %param.25) | copy-start | bytes 388
  8.9 88.0 %copy-start.250 = (s32[2,1,64]{2,1,0:T(1,128)S(1)}, s32[2,1,64]{2,1,0:T(1,128)}, u32[]{:S(2)}) copy-start(s32[2,1,64]{2,1,0:T(1,128)} %param.19) | copy-start | bytes 1540
  10.0 101.0 %copy-start.219 = (f32[1,2304]{1,0:T(1,128)S(1)}, f32[1,2304]{1,0:T(1,128)}, u32[]{:S(2)}) copy-start(f32[1,2304]{1,0:T(1,128)} %param.24) | copy-start | bytes 27652
  10.0 101.6 %slice-start = ((f32[1,2304]{1,0:T(1,128)}), f32[1,256]{1,0:T(1,128)S(1)}, s32[]{:S(2)}) async-start(f32[1,2304]{1,0:T(1,128)} %param.24), calls=%async_computation.5 | async-start | bytes 2048 | tf_op jit(solution)/shard_map/slice | solution.py:245
  11.0 200.3 %copy-start.52 = (bf16[2,1,64,1024]{3,2,1,0:T(8,128)(2,1)S(1)}, bf16[2,1,64,1024]{3,2,1,0:T(8,128)(2,1)}, u32[]{:S(2)}) copy-start(bf16[2,1,64,1024]{3,2,1,0:T(8,128)(2,1)} %param.20) | copy-start | bytes 786436
  11.0 606.4 %reduce-scatter.2.cloned.1.call-start = ((), (), s32[]{:S(2)}) async-start(), calls=%async_computation.2 | async-start | bytes 3604480 | tf_op jit(solution)/shard_map/reduce_scatter | solution.py:552
  11.0 214.8 %collective-permute-start = (bf16[512,1024]{1,0:T(8,128)(2,1)}, bf16[512,1024]{1,0:T(8,128)(2,1)S(1)}, u32[]{:S(2)}, u32[]{:S(2)}) collective-permute-start(bf16[512,1024]{1,0:T(8,128)(2,1)} %bitcast.46), channel_id=1, source_target_pairs={{0,0},{1,4},{2,8},{3,12},{4,1},{5,5},{6,9},{7,13},{8,2},{9,6},{10,... | collective-permute-start | bytes 3145736 | tf_op jit(solution)/shard_map/ppermute | solution.py:466
  13.1 198.9 %copy-start.86 = (f32[1,1024]{1,0:T(1,128)S(1)}, f32[1,1024]{1,0:T(1,128)}, u32[]{:S(2)}) copy-start(f32[1,1024]{1,0:T(1,128)} %param.21) | copy-start | bytes 12292
  97.1 115.8 %copy-start.156 = (f32[256]{0:T(256)}, f32[256]{0:T(256)S(1)}, u32[]{:S(2)}) copy-start(f32[256]{0:T(256)S(1)} %rsqrt.160) | copy-start | bytes 3076
  225.8 244.3 %copy-start.6 = (bf16[512,1024]{1,0:T(8,128)(2,1)}, bf16[512,1024]{1,0:T(8,128)(2,1)S(1)}, u32[]{:S(2)}) copy-start(bf16[512,1024]{1,0:T(8,128)(2,1)S(1)} %collective-permute-done) | copy-start | bytes 3145732
  240.3 12.5 %collective-permute-start.1 = (bf16[64,1024]{1,0:T(8,128)(2,1)S(1)}, bf16[64,1024]{1,0:T(8,128)(2,1)S(1)}, u32[]{:S(2)}, u32[]{:S(2)}) collective-permute-start(bf16[64,1024]{1,0:T(8,128)(2,1)S(1)} %add_convert_fusion.5), channel_id=1, source_target_pairs={{0,16},{1,17},{2,18},{3,19},{4,20},{5,21},{6,22},{7,23},{8,24},{9,... | collective-permute-start | bytes 393224 | tf_op jit(solution)/shard_map/ppermute | solution.py:27
  271.2 52.8 %copy-start.35 = (bf16[256,1408]{0,1:T(8,128)(2,1)}, bf16[256,1408]{0,1:T(8,128)(2,1)S(1)}, u32[]{:S(2)}) copy-start(bf16[256,1408]{0,1:T(8,128)(2,1)S(1)} %get-tuple-element.428) | copy-start | bytes 2162692
  282.6 18.2 %copy-start.261 = (f32[64]{0:T(128)S(1)}, f32[64]{0:T(128)}, u32[]{:S(2)}) copy-start(f32[64]{0:T(128)} %get-tuple-element.252) | copy-start | bytes 772
  282.6 18.8 %copy-start.49 = (bf16[2,1,64,1024]{3,2,1,0:T(8,128)(2,1)S(1)}, bf16[2,1,64,1024]{3,2,1,0:T(8,128)(2,1)}, u32[]{:S(2)}) copy-start(bf16[2,1,64,1024]{3,2,1,0:T(8,128)(2,1)} %param.18) | copy-start | bytes 786436
  296.9 21.3 %copy-start.238 = (f32[64]{0:T(128)}, f32[64]{0:T(128)S(1)}, u32[]{:S(2)}) copy-start(f32[64]{0:T(128)S(1)} %convert_reduce_fusion.13) | copy-start | bytes 772
  296.9 21.6 %copy-start.157 = (f32[256]{0:T(256)S(1)}, f32[256]{0:T(256)}, u32[]{:S(2)}) copy-start(f32[256]{0:T(256)} %copy-done.156) | copy-start | bytes 3076
  296.9 21.6 %copy-start.159 = (f32[256]{0:T(256)S(1)}, f32[256]{0:T(256)}, u32[]{:S(2)}) copy-start(f32[256]{0:T(256)} %copy-done.158) | copy-start | bytes 3076
  299.1 2.3 collective-permute-start.2
  338.4 16.3 %copy-start.231 = (f32[64]{0:T(128)S(1)}, f32[64]{0:T(128)}, u32[]{:S(2)}) copy-start(f32[64]{0:T(128)} %copy-done.230) | copy-start | bytes 772
  338.4 16.3 %copy-start.239 = (f32[64]{0:T(128)S(1)}, f32[64]{0:T(128)}, u32[]{:S(2)}) copy-start(f32[64]{0:T(128)} %copy-done.238) | copy-start | bytes 772
  359.9 16.9 %copy-start.26 = (bf16[256,768]{0,1:T(8,128)(2,1)}, bf16[256,768]{0,1:T(8,128)(2,1)S(1)}, u32[]{:S(2)}) copy-start(bf16[256,768]{0,1:T(8,128)(2,1)S(1)} %get-tuple-element.244) | copy-start | bytes 1179652
  360.0 16.9 %copy-start.78 = (bf16[64,1024]{1,0:T(8,128)(2,1)S(1)}, bf16[64,1024]{1,0:T(8,128)(2,1)}, u32[]{:S(2)}) copy-start(bf16[64,1024]{1,0:T(8,128)(2,1)} %bitcast_convert_fusion.1) | copy-start | bytes 393220
  433.7 17.6 %copy-start.43 = (f32[64,1024]{1,0:T(8,128)S(1)}, f32[64,1024]{1,0:T(8,128)}, u32[]{:S(2)}) copy-start(f32[64,1024]{1,0:T(8,128)} %copy-done.41) | copy-start | bytes 786436
  433.7 17.6 %copy-start.181 = (f32[64]{0:T(128)S(1)}, f32[64]{0:T(128)}, u32[]{:S(2)}) copy-start(f32[64]{0:T(128)} %add_rsqrt_fusion.6) | copy-start | bytes 772
  433.8 17.6 %copy-start.191 = (f32[64]{0:T(128)S(1)}, f32[64]{0:T(128)}, u32[]{:S(2)}) copy-start(f32[64]{0:T(128)} %copy-done.189) | copy-start | bytes 772
  448.1 3.2 collective-permute-start.3
  451.6 18.6 %copy-start.27 = (bf16[256,768]{0,1:T(8,128)(2,1)S(1)}, bf16[256,768]{0,1:T(8,128)(2,1)}, u32[]{:S(2)}) copy-start(bf16[256,768]{0,1:T(8,128)(2,1)} %copy-done.26) | copy-start | bytes 1179652
  479.7 20.8 %copy-start.8 = (f32[254,768]{0,1:T(8,128)S(1)}, f32[254,768]{0,1:T(8,128)}, u32[]{:S(2)}) copy-start(f32[254,768]{0,1:T(8,128)} %copy-done.7) | copy-start | bytes 2340868
  507.2 17.0 %copy-start.258 = (f32[64,1]{0,1:T(1,128)S(1)}, f32[64,1]{0,1:T(1,128)}, u32[]{:S(2)}) copy-start(f32[64,1]{0,1:T(1,128)} %get-tuple-element.235) | copy-start | bytes 772
  507.2 17.0 %copy-start.31 = (bf16[256,768]{0,1:T(8,128)(2,1)S(1)}, bf16[256,768]{0,1:T(8,128)(2,1)}, u32[]{:S(2)}) copy-start(bf16[256,768]{0,1:T(8,128)(2,1)} %get-tuple-element.230) | copy-start | bytes 1179652
  521.9 21.5 %copy-start.67 = (bf16[1,256,8,64]{1,3,2,0:T(8,128)(2,1)S(1)}, bf16[1,256,8,64]{1,3,2,0:T(8,128)(2,1)}, u32[]{:S(2)}) copy-start(bf16[1,256,8,64]{1,3,2,0:T(8,128)(2,1)} %get-tuple-element.341) | copy-start | bytes 786436
  521.9 21.5 %copy-start.122 = (f32[1,512]{1,0:T(1,128)S(1)}, f32[1,512]{1,0:T(1,128)}, u32[]{:S(2)}) copy-start(f32[1,512]{1,0:T(1,128)} %constant_dynamic-slice_fusion) | copy-start | bytes 6148
  521.9 21.5 %copy-start.170 = (f32[256]{0:T(256)S(1)}, f32[256]{0:T(256)}, u32[]{:S(2)}) copy-start(f32[256]{0:T(256)} %copy-done.169) | copy-start | bytes 3076
  522.9 3.2 collective-permute-start.4
  526.2 19.7 %copy-start.79 = (bf16[64,1024]{1,0:T(8,128)(2,1)}, bf16[64,1024]{1,0:T(8,128)(2,1)S(1)}, u32[]{:S(2)}) copy-start(bf16[64,1024]{1,0:T(8,128)(2,1)S(1)} %collective-permute-done.4) | copy-start | bytes 393220
  572.5 101.2 %all-reduce.39.cloned.1.call-start = ((), (), s32[]{:S(2)}) async-start(), calls=%async_computation.3 | async-start | bytes 2097152 | tf_op jit(solution)/shard_map/psum | solution.py:542
  575.2 47.2 %copy-start.5 = (bf16[1024,1408]{0,1:T(8,128)(2,1)S(1)}, bf16[1024,1408]{0,1:T(8,128)(2,1)}, u32[]{:S(2)}) copy-start(bf16[1024,1408]{0,1:T(8,128)(2,1)} %all-gather.4.cloned.1.call-done) | copy-start | bytes 8650756
  575.2 284.7 %all-gather.6.cloned.1.call-start = ((), (), s32[]{:S(2)}) async-start(), calls=%async_computation.4 | async-start | bytes 3604480 | tf_op jit(solution)/shard_map/all_gather | solution.py:553
  622.4 16.4 %copy-start.65 = (bf16[64,1024]{1,0:T(8,128)(2,1)S(1)}, bf16[64,1024]{1,0:T(8,128)(2,1)}, u32[]{:S(2)}) copy-start(bf16[64,1024]{1,0:T(8,128)(2,1)} %get-tuple-element.220) | copy-start | bytes 393220
  624.6 50.9 %copy-start.247 = (f32[1,32]{1,0:T(1,128)S(1)}, f32[1,32]{1,0:T(1,128)}, u32[]{:S(2)}) copy-start(f32[1,32]{1,0:T(1,128)} %param.26) | copy-start | bytes 388
  624.6 232.2 %copy-start.51 = (f32[64,1024]{1,0:T(8,128)S(1)}, f32[64,1024]{1,0:T(8,128)}, u32[]{:S(2)}) copy-start(f32[64,1024]{1,0:T(8,128)} %copy-done.50) | copy-start | bytes 786436
  624.6 232.2 %copy-start.80 = (bf16[64,1024]{1,0:T(8,128)(2,1)S(1)}, bf16[64,1024]{1,0:T(8,128)(2,1)}, u32[]{:S(2)}) copy-start(bf16[64,1024]{1,0:T(8,128)(2,1)} %copy-done.79) | copy-start | bytes 393220
  624.7 232.3 %copy-start.71 = (f32[1,64,1024]{2,1,0:T(8,128)S(1)}, f32[1,64,1024]{2,1,0:T(8,128)}, u32[]{:S(2)}) copy-start(f32[1,64,1024]{2,1,0:T(8,128)} %get-tuple-element.217) | copy-start | bytes 786436
  673.6 184.7 %collective-permute-start.5 = (bf16[512,1024]{1,0:T(8,128)(2,1)}, bf16[512,1024]{1,0:T(8,128)(2,1)S(1)}, u32[]{:S(2)}, u32[]{:S(2)}) collective-permute-start(bf16[512,1024]{1,0:T(8,128)(2,1)} %all-reduce.39.cloned.1.call-done), channel_id=1, source_target_pairs={{0,0},{1,4},{2,8},{3,12},{4,1},{5,5},{6,9},{7,13},{8,2},{9,6},{10,... | collective-permute-start | bytes 3145736 | tf_op jit(solution)/shard_map/ppermute | solution.py:541
  (226 other events, 1084.1 us)
Sparse Core Ops, SparseCore 0:
  11.1 94.5 all-gather.3
  572.6 44.7 reduce-scatter.1
  621.0 52.5 all-reduce.38
  675.1 118.2 all-gather.5

commit v2 on v1

--- a/solution.py
+++ b/solution.py
@@ -65,19 +65,22 @@
     return (grad_chan, jnp.stack(weight_rows), jnp.sum(grad_pre, axis=0))
 
 
-def block_tables(doc_start):
-    spans = doc_start.shape[0] // SPAN
-    starts = doc_start.reshape(spans, SPAN)
+def block_tables(places):
+    spans = places.shape[0] // SPAN
+    local = places.reshape(spans, SPAN)
     inside = lax.iota(jnp.int32, SPAN)
-    causal = (inside[:, None] >= inside[None, :])[None] & (starts[:, :, None] == starts[:, None, :])
-    at_end = starts == starts[:, -1:]
-    at_start = starts == starts[:, :1]
+    gap = inside[:, None] - inside[None, :]
+    causal = (gap >= 0)[None] & (gap[None] <= local[:, :, None])
+    at_end = inside[None, :] >= SPAN - 1 - local[:, -1:]
+    at_start = local >= inside[None, :]
     blocks = lax.iota(jnp.int32, spans)
     between = (
         (blocks[None, :, None] < blocks[None, None, :])
         & (blocks[None, None, :] < blocks[:, None, None])
     ).astype(jnp.float32)
-    across = (starts[None, :, -1] == starts[:, 0][:, None]) & (blocks[None, :] < blocks[:, None])
+    across = (blocks[:, None] * SPAN - local[:, :1] < (blocks[None, :] + 1) * SPAN) & (
+        blocks[None, :] < blocks[:, None]
+    )
     return (causal, at_end, at_start, between, across)
 
 
@@ -125,7 +128,7 @@
     c_blocks = act[:, width * P_SIZE + N :].reshape(spans, SPAN, N)
     steps = jax.nn.softplus(step_raw.astype(jnp.float32) + step_bias)
     step_heads = jnp.swapaxes(steps.reshape(spans, SPAN, width), 1, 2)
-    tables = block_tables(lax.iota(jnp.int32, length) - places)
+    tables = block_tables(places)
     return (pre_act, x_blocks, b_blocks, c_blocks, step_heads, tables)
 
 
@@ -250,14 +253,14 @@
     return (columns, biases, step_bias, rates, skips)
 
 
-def exchange_kernel(size, spread, src, dst, send, recv, here):
-    me = lax.axis_index("seq")
+def exchange_kernel(axis, size, spread, src, dst, send, recv, here):
+    me = lax.axis_index(axis)
     barrier = pltpu.get_barrier_semaphore()
     for distance in range(1, size):
         pl.semaphore_signal(
             barrier,
             inc=1,
-            device_id={"seq": lax.rem(me + distance, size)},
+            device_id={axis: lax.rem(me + distance, size)},
             device_id_type=pl.DeviceIdType.MESH,
         )
     own = pltpu.make_async_copy(src if spread else src.at[me], dst.at[me], here)
@@ -271,7 +274,7 @@
             dst_ref=dst.at[me],
             send_sem=send.at[distance - 1],
             recv_sem=recv.at[distance - 1],
-            device_id={"seq": peer},
+            device_id={axis: peer},
             device_id_type=pl.DeviceIdType.MESH,
         )
         copy.start()
@@ -281,11 +284,11 @@
         copy.wait()
 
 
-def exchange(block, spread, call_id):
-    size = lax.axis_size("seq")
+def exchange(block, spread, call_id, axis="seq"):
+    size = lax.axis_size(axis)
     part = block.shape if spread else block.shape[1:]
     return pl.pallas_call(
-        functools.partial(exchange_kernel, size, spread),
+        functools.partial(exchange_kernel, axis, size, spread),
         out_shape=jax.ShapeDtypeStruct((size,) + part, block.dtype),
         in_specs=[pl.BlockSpec(memory_space=pltpu.VMEM)],
         out_specs=pl.BlockSpec(memory_space=pltpu.VMEM),
@@ -434,7 +437,10 @@
         placed(rate_log, H),
         placed(skip, H),
     ]
-    flat = lax.psum(jnp.concatenate([g.reshape(-1) for g in grads]), ("seq", "wt"))
+    flat = jnp.concatenate([g.reshape(-1) for g in grads])
+    flat = jnp.pad(flat, (0, -flat.shape[0] % 1024)).reshape(-1, 128)
+    flat = jnp.sum(exchange(flat, True, 4, "wt"), axis=0)
+    flat = jnp.sum(exchange(flat, True, 5), axis=0).reshape(-1)
     summed = []
     first = 0
     for grad in grads:
@@ -468,7 +474,10 @@
         w_out = lax.dynamic_slice_in_dim(
             lax.all_gather(out_weight[0], "wt", axis=0, tiled=True), me * inner, inner, 0
         )
-    places_all = lax.all_gather(positions, "seq", axis=2, tiled=True)
+    places_all = [
+        lax.optimization_barrier(gathered.reshape(-1))
+        for gathered in jnp.unstack(lax.all_gather(positions[:, 0], "seq", axis=0), axis=1)
+    ]
     gain = norm_gain[0]
     gate = lax.dynamic_slice_in_dim(gate_gain[0], me * inner, inner, 0)
     heads = head_params(conv_weight[0], conv_bias[0], dt_bias[0], a_log[0], skip_d[0])
@@ -482,8 +491,8 @@
         inputs = jnp.where(first_section, fresh, received)
         places = jnp.where(
             first_section,
-            places_all[min(step_index, batches - 1), 0],
-            places_all[max(step_index - 1, 0), 0],
+            places_all[min(step_index, batches - 1)],
+            places_all[max(step_index - 1, 0)],
         )
         result, kept = forward_tick(inputs, places, w_in, w_out, gain, gate, heads)
         kept_ticks.append(kept)
@@ -550,7 +559,9 @@
         )
     total_out = total_out.astype(jnp.float32)
     shard_in = lax.psum_scatter(weight_grad(in_ticks), "wt", scatter_dimension=0, tiled=True)
-    groups = lax.all_gather(shard_in, "seq", axis=0)
+    summed = sum_small(small_totals)
+    shard_in, summed = lax.optimization_barrier((shard_in, summed))
+    groups = exchange(shard_in, True, 6)
     ends = 2 * inner + 2 * N
     total_in = jnp.concatenate(
         [groups[index, :, :inner] for index in range(seq)]
@@ -563,7 +574,6 @@
         + [groups[index, :, ends : ends + width] for index in range(seq)],
         1,
     ).astype(jnp.float32)
-    summed = sum_small(small_totals)
     section_rows = jnp.stack(
         [
             jnp.where(first_section, out_ticks[index], out_ticks[index + 1])

time: 887 us -> 722 us (0.81)
  the two profiles are of different devices: /device:TPU:0 before, /device:TPU:9 now
where the time goes in v2:
time: 722 us; the launch traced here: 711 us
  Pallas kernels  371 us (51%)
  other arithmetic  126 us (17%)
  matrix products  79.8 us (11%)
  local copies, waits for them, and re-layouts  67.1 us (9%)
  between operations  22.1 us (3%)
  waiting for transfers between devices  21.4 us (3%)
  starting transfers between devices  15.1 us (2%)
  blocking collectives  8.11 us (1%)
    pallas_call x15, Pallas kernels, exchange(): pl.pallas_call(functools.partial(exchange_kernel, axis, size, spread), ou...  371 us
    another operation x36, other arithmetic  22.4 us
    psum x1, waiting for transfers between devices, body(): lax.psum(grad_out_group, 'wt')  14.5 us
  transfers between devices with their start and end apart: 9, of which 4 were waited for; matrix products, arithmetic and copies ran while one was open for 10% of the time, Pallas kernels for 23%

profile of v2, /device:TPU:9, one launch (start us, length us, event | category | flops | bytes accessed | tf_op | source)
XLA Modules:
  0.0 711.2 jit_solution(8893587010036909841)
XLA Ops:
  11.1 3.0 collective-permute-start
  14.1 75.6 %shard_map.203 = bf16[4,64,1024]{2,1,0:T(8,128)(2,1)S(1)} custom-call(bf16[64,1024]{1,0:T(8,128)(2,1)S(1)} %select_bitcast_fusion.2.src), custom_call_target="tpu_custom_call" | custom-call | tf_op jit(solution)/shard_map/pallas_call | solution.py:290
  90.7 8.1 %all-gather = s32[8,1,64]{2,1,0:T(1,128)S(1)} all-gather(s32[2,1,64]{2,1,0:T(1,128)S(1)} %copy-done.264), channel_id=2, replica_groups=mesh['section'=2,'seq'=4,'wt'=4] {'seq'}, dimensions={0}, use_global_device_ids=true | all-gather | bytes 2560 | tf_op jit(solution)/shard_map/all_gather | solution.py:479
  118.2 2.8 fusion.356
  127.7 2.0 fusion.28
  132.0 14.5 %shard_map.204 = bf16[4,64,1152]{2,1,0:T(8,128)(2,1)S(1)} custom-call(bf16[4,64,1152]{2,1,0:T(8,128)(2,1)S(1)} %bitcast.949), custom_call_target="tpu_custom_call" | custom-call | tf_op jit(solution)/shard_map/pallas_call | solution.py:290
  151.7 13.0 %shard_map.205 = bf16[4,64,1024]{2,1,0:T(8,128)(2,1)S(1)} custom-call(bf16[64,1024]{1,0:T(8,128)(2,1)S(1)} %get-tuple-element.240.src), custom_call_target="tpu_custom_call" | custom-call | tf_op jit(solution)/shard_map/pallas_call | solution.py:290
  165.8 3.9 fusion.357
  175.7 2.1 fusion.29
  180.0 14.4 %shard_map.206 = bf16[4,64,1152]{2,1,0:T(8,128)(2,1)S(1)} custom-call(bf16[4,64,1152]{2,1,0:T(8,128)(2,1)S(1)} %bitcast.950), custom_call_target="tpu_custom_call" | custom-call | tf_op jit(solution)/shard_map/pallas_call | solution.py:290
  202.3 13.4 %shard_map.207 = bf16[4,64,1024]{2,1,0:T(8,128)(2,1)S(1)} custom-call(bf16[64,1024]{1,0:T(8,128)(2,1)S(1)} %get-tuple-element.212.src), custom_call_target="tpu_custom_call" | custom-call | tf_op jit(solution)/shard_map/pallas_call | solution.py:290
  215.9 2.0 select_select_fusion.1
  217.9 4.1 fusion.358
  224.5 2.9 multiply_convert_fusion.12
  234.4 3.1 broadcast_select_fusion.17
  237.5 2.0 multiply_reduce_fusion.33
  247.4 16.0 %shard_map.208 = bf16[4,64,1152]{2,1,0:T(8,128)(2,1)S(1)} custom-call(bf16[4,64,1152]{2,1,0:T(8,128)(2,1)S(1)} %bitcast.951), custom_call_target="tpu_custom_call" | custom-call | tf_op jit(solution)/shard_map/pallas_call | solution.py:290
  264.9 3.9 multiply_convert_fusion.13
  276.6 14.4 %shard_map.209 = bf16[4,64,1152]{2,1,0:T(8,128)(2,1)S(1)} custom-call(bf16[64,1152]{1,0:T(8,128)(2,1)S(1)} %fusion.194.src), custom_call_target="tpu_custom_call" | custom-call | tf_op jit(solution)/shard_map/pallas_call | solution.py:290
  292.2 3.9 fusion.103
  303.6 3.1 multiply_reduce_fusion.8
  318.9 2.2 fusion.21
  327.4 2.3 multiply_reduce_fusion.29
  332.7 13.0 %shard_map.210 = bf16[4,64,1024]{2,1,0:T(8,128)(2,1)S(1)} custom-call(bf16[4,64,1024]{2,1,0:T(8,128)(2,1)S(1)} %bitcast.953), custom_call_target="tpu_custom_call" | custom-call | tf_op jit(solution)/shard_map/pallas_call | solution.py:290
  356.5 3.4 collective-permute-start.3
  370.7 15.2 %shard_map.211 = bf16[4,64,1152]{2,1,0:T(8,128)(2,1)S(1)} custom-call(bf16[64,1152]{1,0:T(8,128)(2,1)S(1)} %fusion.195.src), custom_call_target="tpu_custom_call" | custom-call | tf_op jit(solution)/shard_map/pallas_call | solution.py:290
  386.1 2.4 fusion.174
  388.6 3.8 fusion.110
  399.4 3.2 multiply_reduce_fusion.6
  414.8 1.9 fusion.20
  424.5 14.6 %shard_map.212 = bf16[4,64,1024]{2,1,0:T(8,128)(2,1)S(1)} custom-call(bf16[4,64,1024]{2,1,0:T(8,128)(2,1)S(1)} %bitcast.954), custom_call_target="tpu_custom_call" | custom-call | tf_op jit(solution)/shard_map/pallas_call | solution.py:290
  440.1 1.8 select_bitcast_fusion
  441.9 2.5 collective-permute-start.4
  447.0 16.2 %shard_map.213 = bf16[4,64,1152]{2,1,0:T(8,128)(2,1)S(1)} custom-call(bf16[64,1152]{1,0:T(8,128)(2,1)S(1)} %fusion.196.src), custom_call_target="tpu_custom_call" | custom-call | tf_op jit(solution)/shard_map/pallas_call | solution.py:290
  464.5 2.6 fusion.175
  467.1 3.3 fusion.117
  475.0 2.0 multiply_reduce_fusion.4
  492.7 3.4 convolution_convert_fusion
  509.9 2.1 convolution_convert_fusion.5
  512.2 14.4 %shard_map.214 = bf16[4,64,1024]{2,1,0:T(8,128)(2,1)S(1)} custom-call(bf16[4,64,1024]{2,1,0:T(8,128)(2,1)S(1)} %bitcast.952), custom_call_target="tpu_custom_call" | custom-call | tf_op jit(solution)/shard_map/pallas_call | solution.py:290
  529.3 14.5 %all-reduce.40.cloned.1.call-done = bf16[512,1024]{1,0:T(8,128)(2,1)} async-done(((bf16[512,1024]{1,0:T(8,128)(2,1)}), bf16[512,1024]{1,0:T(8,128)(2,1)}) %all-reduce.40.cloned.1.call-update) | async-done | bytes 1048592 | tf_op jit(solution)/shard_map/psum | solution.py:551
  543.8 3.1 collective-permute-start.5
  546.9 52.7 %shard_map.215 = f32[4,120,128]{2,1,0:T(8,128)S(1)} custom-call(f32[120,128]{1,0:T(8,128)S(1)} %pad_bitcast_fusion.src), custom_call_target="tpu_custom_call" | custom-call | tf_op jit(solution)/shard_map/pallas_call | solution.py:290
  599.6 18.5 %shard_map.216 = f32[4,120,128]{2,1,0:T(8,128)S(1)} custom-call(f32[120,128]{1,0:T(8,128)S(1)} %reduce_sum.942.src), custom_call_target="tpu_custom_call" | custom-call | tf_op jit(solution)/shard_map/pallas_call | solution.py:290
  623.5 5.5 reduce-scatter.2.cloned.1.call-done.src
  630.1 65.4 %shard_map.217 = bf16[4,256,1408]{2,1,0:T(8,128)(2,1)S(1)} custom-call(bf16[256,1408]{1,0:T(8,128)(2,1)S(1)} %copy-done.2), custom_call_target="tpu_custom_call" | custom-call | tf_op jit(solution)/shard_map/pallas_call | solution.py:290
  697.4 3.3 concatenate.221
  700.7 2.9 copy.580
  (945 shorter events, 204.7 us)
Async XLA Ops:
  7.2 104.0 %copy-start = (f32[1,2048]{1,0:T(1,128)S(1)}, f32[1,2048]{1,0:T(1,128)}, u32[]{:S(2)}) copy-start(f32[1,2048]{1,0:T(1,128)} %param.28) | copy-start | bytes 24580
  7.2 110.9 %all-gather.3.cloned.1.call-start = ((), (), s32[]{:S(2)}) async-start(), calls=%async_computation.1 | async-start | bytes 3604480 | tf_op jit(solution)/shard_map/all_gather | solution.py:470
  8.9 81.8 %copy-start.264 = (s32[2,1,64]{2,1,0:T(1,128)S(1)}, s32[2,1,64]{2,1,0:T(1,128)}, u32[]{:S(2)}) copy-start(s32[2,1,64]{2,1,0:T(1,128)} %param.19) | copy-start | bytes 1540
  10.0 99.9 %copy-start.277 = (f32[1,32]{1,0:T(1,128)S(1)}, f32[1,32]{1,0:T(1,128)}, u32[]{:S(2)}) copy-start(f32[1,32]{1,0:T(1,128)} %param.26) | copy-start | bytes 388
  10.0 100.6 %copy-start.265 = (f32[1,32]{1,0:T(1,128)S(1)}, f32[1,32]{1,0:T(1,128)}, u32[]{:S(2)}) copy-start(f32[1,32]{1,0:T(1,128)} %param.25) | copy-start | bytes 388
  10.0 100.6 %copy-start.266 = (f32[1,32]{1,0:T(1,128)S(1)}, f32[1,32]{1,0:T(1,128)}, u32[]{:S(2)}) copy-start(f32[1,32]{1,0:T(1,128)} %param.27) | copy-start | bytes 388
  10.0 101.2 %copy-start.232 = (f32[1,2304]{1,0:T(1,128)S(1)}, f32[1,2304]{1,0:T(1,128)}, u32[]{:S(2)}) copy-start(f32[1,2304]{1,0:T(1,128)} %param.24) | copy-start | bytes 27652
  10.0 101.8 %slice-start = ((f32[1,2304]{1,0:T(1,128)}), f32[1,256]{1,0:T(1,128)S(1)}, s32[]{:S(2)}) async-start(f32[1,2304]{1,0:T(1,128)} %param.24), calls=%async_computation.4 | async-start | bytes 2048 | tf_op jit(solution)/shard_map/slice | solution.py:248
  10.0 107.2 %copy-start.52 = (bf16[2,1,64,1024]{3,2,1,0:T(8,128)(2,1)S(1)}, bf16[2,1,64,1024]{3,2,1,0:T(8,128)(2,1)}, u32[]{:S(2)}) copy-start(bf16[2,1,64,1024]{3,2,1,0:T(8,128)(2,1)} %param.20) | copy-start | bytes 786436
  10.1 107.8 %copy-start.87 = (f32[1,1024]{1,0:T(1,128)S(1)}, f32[1,1024]{1,0:T(1,128)}, u32[]{:S(2)}) copy-start(f32[1,1024]{1,0:T(1,128)} %param.21) | copy-start | bytes 12292
  11.0 532.8 %all-reduce.40.cloned.1.call-start = ((), (), s32[]{:S(2)}) async-start(), calls=%async_computation.3 | async-start | bytes 2097152 | tf_op jit(solution)/shard_map/psum | solution.py:551
  11.1 119.6 %collective-permute-start = (bf16[512,1024]{1,0:T(8,128)(2,1)}, bf16[512,1024]{1,0:T(8,128)(2,1)S(1)}, u32[]{:S(2)}, u32[]{:S(2)}) collective-permute-start(bf16[512,1024]{1,0:T(8,128)(2,1)} %bitcast.47), channel_id=1, source_target_pairs={{0,0},{1,4},{2,8},{3,12},{4,1},{5,5},{6,9},{7,13},{8,2},{9,6},{10,... | collective-permute-start | bytes 3145736 | tf_op jit(solution)/shard_map/ppermute | solution.py:472
  90.0 28.1 %copy-start.168 = (f32[256]{0:T(256)}, f32[256]{0:T(256)S(1)}, u32[]{:S(2)}) copy-start(f32[256]{0:T(256)S(1)} %rsqrt.160) | copy-start | bytes 3076
  130.6 114.8 %copy-start.6 = (bf16[512,1024]{1,0:T(8,128)(2,1)}, bf16[512,1024]{1,0:T(8,128)(2,1)S(1)}, u32[]{:S(2)}) copy-start(bf16[512,1024]{1,0:T(8,128)(2,1)S(1)} %collective-permute-done) | copy-start | bytes 3145732
  146.5 49.5 %copy-start.39 = (f32[64,1024]{1,0:T(8,128)}, f32[64,1024]{1,0:T(8,128)S(1)}, u32[]{:S(2)}) copy-start(f32[64,1024]{1,0:T(8,128)S(1)} %convert_reduce_fusion.5) | copy-start | bytes 786436
  146.8 3.6 collective-permute-start.1
  179.9 19.2 %copy-start.279 = (f32[64]{0:T(128)S(1)}, f32[64]{0:T(128)}, u32[]{:S(2)}) copy-start(f32[64]{0:T(128)} %get-tuple-element.238) | copy-start | bytes 772
  179.9 21.0 %copy-start.50 = (bf16[2,1,64,1024]{3,2,1,0:T(8,128)(2,1)S(1)}, bf16[2,1,64,1024]{3,2,1,0:T(8,128)(2,1)}, u32[]{:S(2)}) copy-start(bf16[2,1,64,1024]{3,2,1,0:T(8,128)(2,1)} %param.18) | copy-start | bytes 786436
  194.5 23.5 %copy-start.37 = (f32[64,1024]{1,0:T(8,128)}, f32[64,1024]{1,0:T(8,128)S(1)}, u32[]{:S(2)}) copy-start(f32[64,1024]{1,0:T(8,128)S(1)} %convert_reduce_fusion.4) | copy-start | bytes 786436
  195.2 20.5 %copy-start.226 = (f32[64]{0:T(128)}, f32[64]{0:T(128)S(1)}, u32[]{:S(2)}) copy-start(f32[64]{0:T(128)S(1)} %add_rsqrt_fusion.7) | copy-start | bytes 772
  196.0 21.9 %copy-start.80 = (bf16[64,1024]{1,0:T(8,128)(2,1)}, bf16[64,1024]{1,0:T(8,128)(2,1)S(1)}, u32[]{:S(2)}) copy-start(bf16[64,1024]{1,0:T(8,128)(2,1)S(1)} %get-tuple-element.252) | copy-start | bytes 393220
  197.3 3.6 collective-permute-start.2
  245.5 18.7 %copy-start.243 = (f32[64]{0:T(128)S(1)}, f32[64]{0:T(128)}, u32[]{:S(2)}) copy-start(f32[64]{0:T(128)} %copy-done.242) | copy-start | bytes 772
  245.5 18.7 %copy-start.248 = (f32[64]{0:T(128)S(1)}, f32[64]{0:T(128)}, u32[]{:S(2)}) copy-start(f32[64]{0:T(128)} %copy-done.247) | copy-start | bytes 772
  245.5 19.3 %copy-start.8 = (f32[253,768]{0,1:T(8,128)S(1)}, f32[253,768]{0,1:T(8,128)}, u32[]{:S(2)}) copy-start(f32[253,768]{0,1:T(8,128)} %slice.761) | copy-start | bytes 2331652
  245.5 19.3 %copy-start.10 = (f32[254,768]{0,1:T(8,128)S(1)}, f32[254,768]{0,1:T(8,128)}, u32[]{:S(2)}) copy-start(f32[254,768]{0,1:T(8,128)} %slice.760) | copy-start | bytes 2340868
  245.5 19.2 %copy-start.12 = (f32[255,768]{0,1:T(8,128)S(1)}, f32[255,768]{0,1:T(8,128)}, u32[]{:S(2)}) copy-start(f32[255,768]{0,1:T(8,128)} %slice.759) | copy-start | bytes 2350084
  245.5 19.2 %copy-start.14 = (f32[253,768]{0,1:T(8,128)S(1)}, f32[253,768]{0,1:T(8,128)}, u32[]{:S(2)}) copy-start(f32[253,768]{0,1:T(8,128)} %slice.744) | copy-start | bytes 2331652
  245.5 19.2 %copy-start.16 = (f32[254,768]{0,1:T(8,128)S(1)}, f32[254,768]{0,1:T(8,128)}, u32[]{:S(2)}) copy-start(f32[254,768]{0,1:T(8,128)} %slice.743) | copy-start | bytes 2340868
  245.5 19.2 %copy-start.103 = (f32[768]{0:T(1024)S(1)}, f32[768]{0:T(1024)}, u32[]{:S(2)}) copy-start(f32[768]{0:T(1024)} %get-tuple-element.162) | copy-start | bytes 9220
  245.5 19.2 %copy-start.119 = (f32[768]{0:T(1024)S(1)}, f32[768]{0:T(1024)}, u32[]{:S(2)}) copy-start(f32[768]{0:T(1024)} %pad_maximum_fusion.1) | copy-start | bytes 9220
  245.5 19.2 %copy-start.206 = (pred[256]{0:T(512)(128)(4,1)S(1)}, pred[256]{0:T(512)(128)(4,1)}, u32[]{:S(2)}) copy-start(pred[256]{0:T(512)(128)(4,1)} %get-tuple-element.407) | copy-start | bytes 772
  245.6 19.2 %copy-start.208 = (pred[256]{0:T(512)(128)(4,1)S(1)}, pred[256]{0:T(512)(128)(4,1)}, u32[]{:S(2)}) copy-start(pred[256]{0:T(512)(128)(4,1)} %get-tuple-element.408) | copy-start | bytes 772
  245.6 19.2 %copy-start.210 = (pred[256]{0:T(512)(128)(4,1)S(1)}, pred[256]{0:T(512)(128)(4,1)}, u32[]{:S(2)}) copy-start(pred[256]{0:T(512)(128)(4,1)} %get-tuple-element.245) | copy-start | bytes 772
  245.6 19.2 %copy-start.212 = (pred[256]{0:T(512)(128)(4,1)S(1)}, pred[256]{0:T(512)(128)(4,1)}, u32[]{:S(2)}) copy-start(pred[256]{0:T(512)(128)(4,1)} %get-tuple-element.357) | copy-start | bytes 772
  245.6 19.2 %copy-start.214 = (pred[256]{0:T(512)(128)(4,1)S(1)}, pred[256]{0:T(512)(128)(4,1)}, u32[]{:S(2)}) copy-start(pred[256]{0:T(512)(128)(4,1)} %get-tuple-element.358) | copy-start | bytes 772
  245.6 19.2 %copy-start.224 = (pred[256]{0:T(512)(128)(4,1)S(1)}, pred[256]{0:T(512)(128)(4,1)}, u32[]{:S(2)}) copy-start(pred[256]{0:T(512)(128)(4,1)} %get-tuple-element.230) | copy-start | bytes 772
  272.8 166.5 %copy-start.66 = (bf16[64,1024]{1,0:T(8,128)(2,1)}, bf16[64,1024]{1,0:T(8,128)(2,1)S(1)}, u32[]{:S(2)}) copy-start(bf16[64,1024]{1,0:T(8,128)(2,1)S(1)} %get-tuple-element.225) | copy-start | bytes 393220
  332.7 22.3 %copy-start.54 = (bf16[2,1,64,1024]{3,2,1,0:T(8,128)(2,1)S(1)}, bf16[2,1,64,1024]{3,2,1,0:T(8,128)(2,1)}, u32[]{:S(2)}) copy-start(bf16[2,1,64,1024]{3,2,1,0:T(8,128)(2,1)} %param.20) | copy-start | bytes 786436
  345.7 22.7 %copy-start.40 = (f32[64,1024]{1,0:T(8,128)S(1)}, f32[64,1024]{1,0:T(8,128)}, u32[]{:S(2)}) copy-start(f32[64,1024]{1,0:T(8,128)} %copy-done.39) | copy-start | bytes 786436
  345.8 40.0 %copy-start.41 = (f32[64,1024]{1,0:T(8,128)}, f32[64,1024]{1,0:T(8,128)S(1)}, u32[]{:S(2)}) copy-start(f32[64,1024]{1,0:T(8,128)S(1)} %convert_reduce_fusion.2) | copy-start | bytes 786436
  356.5 12.0 %collective-permute-start.3 = (bf16[64,1024]{1,0:T(8,128)(2,1)}, bf16[64,1024]{1,0:T(8,128)(2,1)S(1)}, u32[]{:S(2)}, u32[]{:S(2)}) collective-permute-start(bf16[64,1024]{1,0:T(8,128)(2,1)} %fusion.328), channel_id=1, source_target_pairs={{16,0},{17,1},{18,2},{19,3},{20,4},{21,5},{22,6},{23,7},{24,8},{25... | collective-permute-start | bytes 393224 | tf_op jit(solution)/shard_map/ppermute | solution.py:27
  424.5 20.0 %copy-start.270 = (f32[64,1]{0,1:T(1,128)S(1)}, f32[64,1]{0,1:T(1,128)}, u32[]{:S(2)}) copy-start(f32[64,1]{0,1:T(1,128)} %get-tuple-element.223) | copy-start | bytes 772
  424.5 20.0 %copy-start.28 = (bf16[256,768]{0,1:T(8,128)(2,1)S(1)}, bf16[256,768]{0,1:T(8,128)(2,1)}, u32[]{:S(2)}) copy-start(bf16[256,768]{0,1:T(8,128)(2,1)} %get-tuple-element.215) | copy-start | bytes 1179652
  441.9 4.0 collective-permute-start.4
  488.2 140.8 %reduce-scatter.2.cloned.1.call-start = ((), (), s32[]{:S(2)}) async-start(), calls=%async_computation.2 | async-start | bytes 3604480 | tf_op jit(solution)/shard_map/reduce_scatter | solution.py:561
  526.8 91.9 %copy-start.74 = (f32[1,64,1024]{2,1,0:T(8,128)S(1)}, f32[1,64,1024]{2,1,0:T(8,128)}, u32[]{:S(2)}) copy-start(f32[1,64,1024]{2,1,0:T(8,128)} %get-tuple-element.208) | copy-start | bytes 786436
  543.8 78.2 %collective-permute-start.5 = (bf16[512,1024]{1,0:T(8,128)(2,1)}, bf16[512,1024]{1,0:T(8,128)(2,1)S(1)}, u32[]{:S(2)}, u32[]{:S(2)}) collective-permute-start(bf16[512,1024]{1,0:T(8,128)(2,1)} %all-reduce.40.cloned.1.call-done), channel_id=1, source_target_pairs={{0,0},{1,4},{2,8},{3,12},{4,1},{5,5},{6,9},{7,13},{8,2},{9,6},{10,... | collective-permute-start | bytes 3145736 | tf_op jit(solution)/shard_map/ppermute | solution.py:550
  (242 other events, 1314.2 us)
Sparse Core Ops, SparseCore 0:
  11.1 81.4 all-gather.2
  488.3 55.4 all-reduce.39
  547.4 81.5 reduce-scatter.1
